TPU v7x, 32 devices: a whole 2x2x4 slice. The times are simulated.
32 devices in a mesh: tile: 8 (over z, y), head: 4 (over x, core).
Axes of the slice: x: 2, y: 2, z: 4, core: 2. Of those that a mesh axis runs over, the one named last changes fastest.
Arguments:
- tokens: bfloat16 [3072, 3072], P('tile'), may hold values from -200 to 200
- mod_shift: float32 [3072], replicated, may hold values from -3 to 3
- mod_scale: float32 [3072], replicated, may hold values from -2.5 to 2.5
- mod_gate: float32 [3072], replicated, may hold values from -4 to 4
- qkv_weight: bfloat16 [3072, 1536], P(None, 'head'), may hold values from -1 to 1
- out_weight: bfloat16 [512, 3072], P('head'), may hold values from -0.25 to 0.25
- teacher: bfloat16 [3072, 3072], P('tile'), may hold values from -6 to 6
- slot_tiles: int32 [8], replicated, may hold values from 0 to 7, each once
Outputs:
- qkv_grad: float32 [3072, 1536], P('tile', 'head')
- out_grad: float32 [512, 3072], P('head', 'tile')
Inputs may be any that keep to these rules, and one draw needn't show every extreme that they name: Slot s, rows s * 384 to (s + 1) * 384 - 1 of tokens and teacher, holds tile slot_tiles[s]; every tile once.
All inputs are finite; a program needn't handle non-finite values.
Results may differ from a plain program's by a relative error of at most 0.00049.
Values may be sent and summed in bfloat16 or wider, within the bound.
No kernel may reach another device: no remote copies, remote signals or barrier semaphores. Data moves between devices by JAX's collectives and lax.ppermute only.
A program may use at most 128 MiB of HBM per device.

v0:
```python
import math

import jax
import jax.numpy as jnp
from jax import lax
from jax.sharding import PartitionSpec as P

HD = 128
TOK_TILE = 384
TT = 1
TH = 4


EPS_NORM = 1e-05
EPS_ROOT = 1e-06
LOSS_WEIGHT = 32.0


def modulated_norm(tokens, mod_shift, mod_scale):
    values_in = tokens.astype(jnp.float32)
    center = values_in - jnp.mean(values_in, -1, keepdims=True)
    spread = jnp.mean(center * center, -1, keepdims=True)
    return (center * lax.rsqrt(spread + EPS_NORM) * (1.0 + mod_scale) + mod_shift).astype(
        jnp.bfloat16
    )


def root_norm(values):
    factor = lax.rsqrt(jnp.mean(values * values, -1, keepdims=True) + EPS_ROOT)
    return (values * factor, factor)


def root_norm_back(grad_unit, unit_value, factor):
    return factor * (grad_unit - unit_value * jnp.mean(grad_unit * unit_value, -1, keepdims=True))


def tiles_of(slot_tiles, slot_ids):
    onehot = (
        slot_ids[:, None] == jnp.arange(slot_tiles.shape[0], dtype=jnp.int32)[None, :]
    ).astype(jnp.int32)
    return jnp.sum(onehot * slot_tiles[None, :], 1)


def near_tiles(first_tiles, second_tiles, width_tiles):

    def coords(ids):
        return (ids // (TH * width_tiles), ids // width_tiles % TH, ids % width_tiles)

    ta, ha, wa = coords(first_tiles[:, None])
    tb, hb, wb = coords(second_tiles[None, :])
    close = (jnp.abs(ta - tb) <= 1) & (jnp.abs(ha - hb) <= 1) & (jnp.abs(wa - wb) <= 1)
    return close.astype(jnp.float32)


def masked_exp(queries, keys, tile_mask, group_rows):
    att_scale = 1.0 / math.sqrt(HD)
    scores = (
        jnp.einsum("qhd,khd->hqk", queries, keys, preferred_element_type=jnp.float32) * att_scale
    )
    head_count, query_count, key_count = scores.shape
    shaped = jnp.exp(scores).reshape(
        head_count, query_count // group_rows, group_rows, key_count // TOK_TILE, TOK_TILE
    )
    shaped = shaped * tile_mask[None, :, None, :, None]
    return shaped.reshape(head_count, query_count, key_count)


def per_device(tokens, mod_shift, mod_scale, mod_gate, qkv_weight, out_weight, teacher, slot_tiles):
    tok_rows = tokens.shape[0]
    local_tiles = tok_rows // TOK_TILE
    head_count = out_weight.shape[0] // HD
    width_tiles = slot_tiles.shape[0] // (TT * TH)
    att_scale = 1.0 / math.sqrt(HD)
    normed = modulated_norm(tokens, mod_shift, mod_scale)
    projected = jnp.dot(normed, qkv_weight, preferred_element_type=jnp.float32).reshape(
        tok_rows, head_count, 3, HD
    )
    query_unit, query_factor = root_norm(projected[:, :, 0])
    key_unit, key_factor = root_norm(projected[:, :, 1])
    query_b = query_unit.astype(jnp.bfloat16)
    key_b = key_unit.astype(jnp.bfloat16)
    value_b = projected[:, :, 2].astype(jnp.bfloat16)
    all_keys, all_values = (
        lax.all_gather(key_b, "tile", axis=0, tiled=True),
        lax.all_gather(value_b, "tile", axis=0, tiled=True),
    )
    my_slots = lax.axis_index("tile") * local_tiles + jnp.arange(local_tiles, dtype=jnp.int32)
    my_tiles = tiles_of(slot_tiles, my_slots)
    tile_mask = near_tiles(my_tiles, slot_tiles, width_tiles)
    exp_scores = masked_exp(query_b, all_keys, tile_mask, TOK_TILE)
    totals = jnp.sum(exp_scores, -1)
    att_probs = exp_scores / totals[:, :, None]
    probs_b = att_probs.astype(jnp.bfloat16)
    attended = jnp.einsum(
        "hqk,khd->qhd", probs_b, all_values, preferred_element_type=jnp.float32
    ).astype(jnp.bfloat16)
    flat_att = attended.reshape(tok_rows, head_count * HD)
    partial_branch = jnp.dot(flat_att, out_weight, preferred_element_type=jnp.float32)
    whole_branch = lax.psum(partial_branch, "head")
    residual = LOSS_WEIGHT * (mod_gate * whole_branch - teacher.astype(jnp.float32))
    grad_branch = (mod_gate * residual).astype(jnp.bfloat16)
    contract_rows = (((0,), (0,)), ((), ()))
    out_term = lax.dot_general(
        flat_att, grad_branch, contract_rows, preferred_element_type=jnp.float32
    )
    grad_att = lax.dot_general(
        grad_branch, out_weight, (((1,), (1,)), ((), ())), preferred_element_type=jnp.float32
    )
    grad_att = grad_att.reshape(tok_rows, head_count, HD).astype(jnp.bfloat16)
    row_delta = jnp.sum(grad_att.astype(jnp.float32) * attended.astype(jnp.float32), -1)
    grad_probs = jnp.einsum(
        "qhd,khd->hqk", grad_att, all_values, preferred_element_type=jnp.float32
    )
    grad_scores = (att_probs * (grad_probs - row_delta.T[:, :, None])).astype(jnp.bfloat16)
    grad_query_unit = (
        jnp.einsum("hqk,khd->qhd", grad_scores, all_keys, preferred_element_type=jnp.float32)
        * att_scale
    )
    key_terms = (
        jnp.einsum("hqk,qhd->khd", grad_scores, query_b, preferred_element_type=jnp.float32)
        * att_scale
    )
    value_terms = jnp.einsum("hqk,qhd->khd", probs_b, grad_att, preferred_element_type=jnp.float32)
    grad_key_unit, grad_value = (
        lax.psum_scatter(key_terms, "tile", scatter_dimension=0, tiled=True),
        lax.psum_scatter(value_terms, "tile", scatter_dimension=0, tiled=True),
    )
    grad_query = root_norm_back(grad_query_unit, query_unit, query_factor)
    grad_key = root_norm_back(grad_key_unit, key_unit, key_factor)
    grad_qkv = (
        jnp.stack([grad_query, grad_key, grad_value], 2)
        .astype(jnp.bfloat16)
        .reshape(tok_rows, head_count * 3 * HD)
    )
    qkv_term = lax.dot_general(normed, grad_qkv, contract_rows, preferred_element_type=jnp.float32)
    qkv_grad, out_grad = (
        lax.psum_scatter(qkv_term, "tile", scatter_dimension=0, tiled=True),
        lax.psum_scatter(out_term, "tile", scatter_dimension=1, tiled=True),
    )
    return (qkv_grad, out_grad)


def solution(mesh):
    return jax.shard_map(
        per_device,
        mesh=mesh,
        in_specs=(
            P("tile", None),
            P(),
            P(),
            P(),
            P(None, "head"),
            P("head", None),
            P("tile", None),
            P(),
        ),
        out_specs=(P("tile", "head"), P("head", "tile")),
        check_vma=False,
    )
```

profile of v0, /device:TPU:0, one launch (start us, length us, event | category | flops | bytes accessed | tf_op | source)
XLA Modules:
  0.0 505.7 jit_solution(5379372191616345241)
XLA Ops:
  7.2 0.0 copy-start
  7.2 0.0 copy-start.11
  7.2 0.0 copy-start.13
  7.2 0.0 all-reduce.2.cloned.1.call-start
  7.2 0.0 copy-start.2
  7.3 1.4 fusion.31
  11.3 2.1 convert_reduce_fusion
  13.4 2.4 fusion.2
  15.8 0.0 copy-done.11
  15.8 0.0 copy-done
  15.9 0.0 copy-done.13
  15.9 0.0 copy-done.2
  15.9 0.0 copy-start.12
  15.9 1.7 fusion.39
  17.6 0.0 copy-start.5
  17.7 0.0 copy-done.12
  17.7 0.1 mul.242
  17.8 0.6 copy-done.5
  18.4 33.9 %all_gather.6 = bf16[3072,1,128]{0,2,1:T(8,128)(2,1)S(1)} all-gather(bf16[384,1,128]{0,2,1:T(8,128)(2,1)S(1)} %fusion.21), channel_id=1, replica_groups=mesh['tile'=8,'head'=4] {'tile'}, dimensions={0}, use_global_device_ids=true | all-gather | bytes 884736 | tf_op jit(solution)/shard_map/all_gather | solution.py:84
  52.3 32.3 %all-gather = bf16[3072,1,1,128]{0,3,2,1:T(8,128)(2,1)S(1)} all-gather(bf16[384,1,1,128]{0,3,2,1:T(8,128)(2,1)S(1)} %slice.40), channel_id=2, replica_groups=mesh['tile'=8,'head'=4] {'tile'}, dimensions={0}, use_global_device_ids=true | all-gather | bytes 884736 | tf_op jit(solution)/shard_map/all_gather | solution.py:85
  84.6 0.0 copy-start.8
  84.6 2.4 fusion.41
  86.9 0.0 copy-start.4
  86.9 0.0 copy-start.6
  86.9 0.9 fusion.11
  87.9 0.0 copy-done.8
  87.9 1.2 copy-done.4
  89.1 0.0 copy-done.6
  89.1 0.0 copy-start.10
  89.1 3.0 fusion.27
  92.1 0.0 all-reduce.2.cloned.1.call-update
  92.1 0.0 reduce-scatter.5.cloned.1.call-start
  92.2 0.0 copy-done.10
  92.2 95.3 %all-reduce.2.cloned.1.call-done = f32[384,3072]{1,0:T(8,128)} async-done(((f32[384,3072]{1,0:T(8,128)}), f32[384,3072]{1,0:T(8,128)}) %all-reduce.2.cloned.1.call-update) | async-done | bytes 4718608 | tf_op jit(solution)/shard_map/psum | solution.py:99
  187.4 0.0 copy-start.7
  187.4 0.0 copy-start.9
  187.4 3.9 multiply_convert_fusion.1
  191.4 0.0 copy-done.7
  191.4 0.0 copy-start.3
  191.4 0.8 fusion.18
  192.3 0.0 copy-done.9
  192.3 3.2 multiply_convert_fusion
  195.5 0.0 copy-done.3
  195.5 0.0 copy-start.1
  195.5 1.4 copy-done.1
  196.9 2.7 fusion.6
  199.6 0.0 reduce-scatter.5.cloned.1.call-update
  199.7 0.0 reduce-scatter.7.cloned.1.call-start
  199.7 4.2 convolution_bitcast_fusion
  203.9 0.0 reduce-scatter.7.cloned.1.call-update
  203.9 0.0 reduce-scatter.11.cloned.1.call-start
  204.0 3.4 fusion.25
  207.4 0.0 reduce-scatter.11.cloned.1.call-update
  207.4 0.2 reduce-scatter.9.cloned.1.call-start
  207.6 57.2 %reduce-scatter.5.cloned.1.call-done = f32[384,1,128]{0,2,1:T(8,128)} async-done(((f32[3072,1,128]{0,2,1:T(8,128)}), f32[384,1,128]{0,2,1:T(8,128)}) %reduce-scatter.5.cloned.1.call-update) | async-done | bytes 196624 | tf_op jit(solution)/shard_map/reduce_scatter | solution.py:125
  264.8 2.7 multiply_reduce_fusion.1
  267.5 64.9 %reduce-scatter.7.cloned.1.call-done = f32[384,1,128]{0,2,1:T(8,128)} async-done(((f32[3072,1,128]{0,2,1:T(8,128)}), f32[384,1,128]{0,2,1:T(8,128)}) %reduce-scatter.7.cloned.1.call-update) | async-done | bytes 196624 | tf_op jit(solution)/shard_map/reduce_scatter | solution.py:126
  332.4 0.9 convert_bitcast_fusion
  333.4 1.2 fusion.23
  334.6 5.6 %fusion.37 = f32[3072,384]{1,0:T(8,128)} fusion(bf16[384,384]{0,1:T(8,128)(2,1)S(1)} %bitcast.99, bf16[384,3072]{1,0:T(8,128)(2,1)} %param.8, f32[3072]{0:T(1024)S(1)} %copy-done.13, f32[3072]{0:T(1024)S(1)} %broadcast_add_fusion, f32[384]{0:T(512)S(1)} %add_rsqrt_fusion.2, f32[384]{0:T(512)S(1)} %broadcast_multiply_fusion.3), kind=kOutput, calls=%fused_computation.77 | convolution fusion | flops 913047552 | bytes 7400448 | tf_op jit(solution)/shard_map/dot_general | solution.py:135
  340.2 0.0 reduce-scatter.9.cloned.1.call-update
  340.2 59.8 %reduce-scatter.11.cloned.1.call-done = f32[128,384]{1,0:T(8,128)} async-done(((f32[128,3072]{1,0:T(8,128)}), f32[128,384]{1,0:T(8,128)}) %reduce-scatter.11.cloned.1.call-update) | async-done | bytes 196624 | tf_op jit(solution)/shard_map/reduce_scatter | solution.py:138
  400.0 99.2 %reduce-scatter.9.cloned.1.call-done = f32[384,384]{1,0:T(8,128)} async-done(((f32[3072,384]{1,0:T(8,128)}), f32[384,384]{1,0:T(8,128)}) %reduce-scatter.9.cloned.1.call-update) | async-done | bytes 589840 | tf_op jit(solution)/shard_map/reduce_scatter | solution.py:137
  (13 shorter events, 0.2 us)
Async XLA Ops:
  7.2 8.7 %copy-start = (bf16[3072,384]{1,0:T(8,128)(2,1)S(1)}, bf16[3072,384]{1,0:T(8,128)(2,1)}, u32[]{:S(2)}) copy-start(bf16[3072,384]{1,0:T(8,128)(2,1)} %param.12) | copy-start | bytes 7077892
  7.2 8.6 %copy-start.11 = (f32[3072]{0:T(1024)S(1)}, f32[3072]{0:T(1024)}, u32[]{:S(2)}) copy-start(f32[3072]{0:T(1024)} %param.10) | copy-start | bytes 36868
  7.2 8.7 %copy-start.13 = (f32[3072]{0:T(1024)S(1)}, f32[3072]{0:T(1024)}, u32[]{:S(2)}) copy-start(f32[3072]{0:T(1024)} %param.9) | copy-start | bytes 36868
  7.2 180.2 %all-reduce.2.cloned.1.call-start = ((), (), s32[]{:S(2)}) async-start(), calls=%async_computation.4 | async-start | bytes 9437184 | tf_op jit(solution)/shard_map/psum | solution.py:99
  7.2 8.6 %copy-start.2 = (bf16[384,3072]{1,0:T(8,128)(2,1)S(1)}, bf16[384,3072]{1,0:T(8,128)(2,1)}, u32[]{:S(2)}) copy-start(bf16[384,3072]{1,0:T(8,128)(2,1)} %param.8) | copy-start | bytes 7077892
  15.9 1.8 copy-start.12
  17.6 0.8 copy-start.5
  84.6 3.3 copy-start.8
  86.9 2.1 copy-start.4
  86.9 2.1 copy-start.6
  89.1 3.1 copy-start.10
  92.1 172.7 %reduce-scatter.5.cloned.1.call-start = ((), (), s32[]{:S(2)}) async-start(), calls=%async_computation.5 | async-start | bytes 1769472 | tf_op jit(solution)/shard_map/reduce_scatter | solution.py:125
  187.4 4.0 copy-start.7
  187.4 4.8 copy-start.9
  191.4 4.0 copy-start.3
  195.5 1.4 copy-start.1
  199.7 132.8 %reduce-scatter.7.cloned.1.call-start = ((), (), s32[]{:S(2)}) async-start(), calls=%async_computation.6 | async-start | bytes 1769472 | tf_op jit(solution)/shard_map/reduce_scatter | solution.py:126
  203.9 196.1 %reduce-scatter.11.cloned.1.call-start = ((), (), s32[]{:S(2)}) async-start(), calls=%async_computation.8 | async-start | bytes 1769472 | tf_op jit(solution)/shard_map/reduce_scatter | solution.py:138
  207.4 291.8 %reduce-scatter.9.cloned.1.call-start = ((), (), s32[]{:S(2)}) async-start(), calls=%async_computation.7 | async-start | bytes 5308416 | tf_op jit(solution)/shard_map/reduce_scatter | solution.py:137
Sparse Core Ops, SparseCore 0:
  92.2 95.1 all-reduce.1
  199.8 65.0 reduce-scatter.4
  268.6 63.7 reduce-scatter.6
  336.3 63.6 reduce-scatter.10
  404.5 94.6 reduce-scatter.8
where the time goes:
time: 506 us
  waiting for transfers between devices  376 us (74%)
  blocking collectives  66.1 us (13%)
  matrix products  30.5 us (6%)
  between operations  16.7 us (3%)
  other arithmetic  12.2 us (2%)
    reduce_scatter x1, waiting for transfers between devices, per_device(): lax.psum_scatter(qkv_term, 'tile', scatter_dimension=0, tiled=True)  99.2 us
    psum x1, waiting for transfers between devices, per_device(): whole_branch = lax.psum(partial_branch, 'head')  95.3 us
    reduce_scatter x1, waiting for transfers between devices, per_device(): lax.psum_scatter(value_terms, 'tile', scatter_dimension=0, tiled=True)  64.9 us
    reduce_scatter x1, waiting for transfers between devices, per_device(): lax.psum_scatter(out_term, 'tile', scatter_dimension=1, tiled=True)  59.8 us
    reduce_scatter x1, waiting for transfers between devices, per_device(): lax.psum_scatter(key_terms, 'tile', scatter_dimension=0, tiled=True)  57.2 us
    all_gather x1, blocking collectives, per_device(): lax.all_gather(key_b, 'tile', axis=0, tiled=True)  33.9 us
    all_gather x1, blocking collectives, per_device(): lax.all_gather(value_b, 'tile', axis=0, tiled=True)  32.3 us
  transfers between devices with their start and end apart: 5, of which 5 were waited for; matrix products, arithmetic and copies ran while one was open for 4% of the time, Pallas kernels for 0%

commit v1 on v0

v1 whole, which is shorter than its diff:
```python
import functools
import math

import jax
import jax.numpy as jnp
import numpy as np
from jax import lax
from jax.experimental import pallas as pl
from jax.experimental.pallas import tpu as pltpu
from jax.sharding import PartitionSpec as P

HD = 128
TOK_TILE = 384
LANE_ROWS = TOK_TILE // HD
TT = 1
TH = 4


EPS_NORM = 1e-05
EPS_ROOT = 1e-06
LOSS_WEIGHT = 32.0
EXP_SCALE = math.log2(math.e) / math.sqrt(HD)
ATT_SCALE = 1.0 / math.sqrt(HD)
STAT_ROWS = 32
VMEM_BYTES = 56 * 1024 * 1024

NN = (((1,), (0,)), ((), ()))
NT = (((1,), (1,)), ((), ()))
TN = (((0,), (0,)), ((), ()))


def mm(a, b, dims):
    return lax.dot_general(a, b, dims, preferred_element_type=jnp.float32)


def ring_order(count):
    return [*range(0, count, 2), *range(count - 1 - (count % 2), 0, -2)]


def rel_offsets(count):
    offsets = [0]
    for step in range(1, count // 2 + 1):
        offsets.append(-step)
        if len(offsets) < count:
            offsets.append(step)
    return offsets[:count]


def ring_tables(count):
    order = ring_order(count)
    pos = [order.index(slot) for slot in range(count)]
    rels = rel_offsets(count)
    source = [[order[(pos[s] + rel) % count] for rel in rels] for s in range(count)]
    target = [[order[(pos[s] - rel) % count] for rel in rels] for s in range(count)]
    return np.array(source, np.int32), np.array(target, np.int32)


def shift_perm(count, offset):
    order = ring_order(count)
    return [(order[p], order[(p + offset) % count]) for p in range(count)]


def ring_gather(block, count):
    up, down = [block], [block]
    for _ in range(count // 2):
        up.append(lax.ppermute(up[-1], "tile", shift_perm(count, 1)))
    for _ in range((count - 1) // 2):
        down.append(lax.ppermute(down[-1], "tile", shift_perm(count, -1)))
    out = []
    for rel in rel_offsets(count):
        out.append(up[-rel] if rel <= 0 else down[rel])
    return out


def xor_perm(count, mask):
    return [(h, h ^ mask) for h in range(count)]


def head_gather_doubling(block, count):
    blocks = [block]
    mask = count // 2
    masks = [0]
    while mask:
        moved = [lax.ppermute(b, "head", xor_perm(count, mask)) for b in blocks]
        blocks = blocks + moved
        masks = masks + [m ^ mask for m in masks]
        mask //= 2
    return [blocks[masks.index(m)] for m in range(count)]


def head_gather_direct(block, count):
    return [block] + [lax.ppermute(block, "head", xor_perm(count, m)) for m in range(1, count)]


def near_tiles(first_tiles, second_tiles, width_tiles):

    def coords(ids):
        return (ids // (TH * width_tiles), ids // width_tiles % TH, ids % width_tiles)

    ta, ha, wa = coords(first_tiles[:, None])
    tb, hb, wb = coords(second_tiles[None, :])
    close = (jnp.abs(ta - tb) <= 1) & (jnp.abs(ha - hb) <= 1) & (jnp.abs(wa - wb) <= 1)
    return close.astype(jnp.int32)


def split3(row):
    hi = row.astype(jnp.bfloat16).astype(jnp.float32)
    rest = row - hi
    mid = rest.astype(jnp.bfloat16).astype(jnp.float32)
    return [hi, mid, rest - mid]


def pack_rows(rows):
    pieces = [part for row in rows for part in split3(row)]
    pieces.append(jnp.zeros((STAT_ROWS - len(pieces), HD), jnp.float32))
    return jnp.concatenate(pieces, 0).astype(jnp.bfloat16)


def unpack_rows(packed, index):
    wide = packed.astype(jnp.float32)
    rows = []
    for chunk in range(LANE_ROWS):
        at = (index * LANE_ROWS + chunk) * 3
        rows.append(wide[at : at + 1] + wide[at + 1 : at + 2] + wide[at + 2 : at + 3])
    return jnp.concatenate(rows, 1)


def lane_chunks(row):
    return [row[:, c * HD : (c + 1) * HD] for c in range(LANE_ROWS)]


def project_kernel(tok_ref, shift_ref, scale_ref, w_ref, normed_ref, kv_ref, q_ref):
    query_rows, key_rows = [], []
    for chunk in range(LANE_ROWS):
        rows = pl.ds(chunk * HD, HD)
        values_in = tok_ref[rows, :].astype(jnp.float32)
        center = values_in - jnp.mean(values_in, -1, keepdims=True)
        spread = jnp.mean(center * center, -1, keepdims=True)
        normed = (
            center * lax.rsqrt(spread + EPS_NORM) * (1.0 + scale_ref[...]) + shift_ref[...]
        ).astype(jnp.bfloat16)
        normed_ref[rows, :] = normed
        projected = mm(normed, w_ref[...], NN)
        query, key, value = (projected[:, c * HD : (c + 1) * HD] for c in range(3))
        rq = lax.rsqrt(jnp.mean(query * query, -1, keepdims=True) + EPS_ROOT)
        rk = lax.rsqrt(jnp.mean(key * key, -1, keepdims=True) + EPS_ROOT)
        query, key = query * rq, key * rk
        query_b, key_b = query.astype(jnp.bfloat16), key.astype(jnp.bfloat16)
        q_ref[rows, :] = query_b
        q_ref[pl.ds(TOK_TILE + chunk * HD, HD), :] = (
            query - query_b.astype(jnp.float32)
        ).astype(jnp.bfloat16)
        q_ref[pl.ds(2 * TOK_TILE + chunk * HD, HD), :] = (
            key - key_b.astype(jnp.float32)
        ).astype(jnp.bfloat16)
        kv_ref[rows, :] = key_b
        kv_ref[pl.ds(TOK_TILE + chunk * HD, HD), :] = value.astype(jnp.bfloat16)
        query_rows.append(jnp.broadcast_to(rq, (HD, HD)).T[0:1])
        key_rows.append(jnp.broadcast_to(rk, (HD, HD)).T[0:1])
    q_ref[pl.ds(3 * TOK_TILE, STAT_ROWS), :] = pack_rows(query_rows + key_rows)


def attend_kernel(count, allowed_ref, q_ref, *refs):
    kv_refs = refs[:count]
    att_ref, inv_ref, expo, totals, acc = refs[count:]
    query = q_ref[pl.ds(0, TOK_TILE), :]
    totals[...] = jnp.zeros_like(totals)
    acc[...] = jnp.zeros_like(acc)
    for r in range(count):

        @pl.when(allowed_ref[0, r] != 0)
        def _():
            scores = mm(kv_refs[r][pl.ds(0, TOK_TILE), :], query, NT)
            part = jnp.exp2(scores * EXP_SCALE)
            expo[r] = part
            totals[...] += jnp.sum(part, 0, keepdims=True)

    inverse = 1.0 / totals[...]
    inv_ref[...] = inverse
    for r in range(count):

        @pl.when(allowed_ref[0, r] != 0)
        def _():
            probs = (expo[r] * inverse).astype(jnp.bfloat16)
            acc[...] += mm(kv_refs[r][pl.ds(TOK_TILE, TOK_TILE), :], probs, TN)

    att_ref[...] = acc[...].T.astype(jnp.bfloat16)


def branch_kernel(heads, inv_ref, gate_ref, teacher_ref, *refs):
    att_refs = refs[:heads]
    w_refs = refs[heads : 2 * heads]
    ga_ref, out_ref, acc = refs[2 * heads :]
    step = pl.program_id(0)

    @pl.when(step == 0)
    def _():
        acc[...] = jnp.zeros_like(acc)

    branch = mm(att_refs[0][...], w_refs[0][...], NN)
    for h in range(1, heads):
        branch += mm(att_refs[h][...], w_refs[h][...], NN)
    gate = gate_ref[...]
    residual = LOSS_WEIGHT * (gate * branch - teacher_ref[...].astype(jnp.float32))
    grad = (gate * residual).astype(jnp.bfloat16)
    out_ref[...] = mm(att_refs[0][...], grad, TN)
    acc[...] += mm(grad, w_refs[0][...], NT)

    @pl.when(step == pl.num_programs(0) - 1)
    def _():
        grad_att = acc[...].astype(jnp.bfloat16)
        ga_ref[pl.ds(0, TOK_TILE), :] = grad_att
        product = grad_att.astype(jnp.float32) * att_refs[0][...].astype(jnp.float32)
        delta = jnp.sum(product.T, 0, keepdims=True)
        ga_ref[pl.ds(TOK_TILE, STAT_ROWS), :] = pack_rows(
            lane_chunks(inv_ref[...]) + lane_chunks(delta)
        )


def backward_kernel(count, allowed_ref, *refs):
    kv_in, q_in, ga_in = refs[:count], refs[count : 2 * count], refs[2 * count : 3 * count]
    nb_in = refs[3 * count]
    out_ref = refs[3 * count + 1]
    kv, qq, ga, nb, dq, dk, dv, grads, sems = refs[3 * count + 2 :]
    copies = []
    for r in range(count):
        copies.append(pltpu.make_async_copy(kv_in[r], kv.at[r], sems.at[3 * r]))
        copies.append(pltpu.make_async_copy(q_in[r], qq.at[r], sems.at[3 * r + 1]))
        copies.append(pltpu.make_async_copy(ga_in[r], ga.at[r], sems.at[3 * r + 2]))
    copies.append(pltpu.make_async_copy(nb_in, nb, sems.at[3 * count]))
    for copy in copies:
        copy.start()
    dk[...] = jnp.zeros_like(dk)
    dv[...] = jnp.zeros_like(dv)
    for copy in copies:
        copy.wait()
    first = pl.ds(0, TOK_TILE)
    second = pl.ds(TOK_TILE, TOK_TILE)
    stats = pl.ds(TOK_TILE, STAT_ROWS)

    def per_query(i, carry):
        query = qq[i, first, :]
        grad = ga[i, first, :]
        packed = ga[i, stats, :]
        inverse, delta = unpack_rows(packed, 0), unpack_rows(packed, 1)
        dq[...] = jnp.zeros_like(dq)

        def per_key(j, carry):
            @pl.when(allowed_ref[i, j] != 0)
            def _():
                key = kv[j, first, :]
                value = kv[j, second, :]
                scores = mm(key, query, NT)
                probs = jnp.exp2(scores * EXP_SCALE) * inverse
                grad_probs = mm(value, grad, NT)
                grad_scores = (probs * (grad_probs - delta)).astype(jnp.bfloat16)
                dv[j] += mm(probs.astype(jnp.bfloat16), grad, NN)
                dk[j] += mm(grad_scores, query, NN)
                dq[...] += mm(key, grad_scores, TN)

            return carry

        lax.fori_loop(0, count, per_key, 0)
        query_unit = query.astype(jnp.float32) + qq[i, second, :].astype(jnp.float32)
        factor = unpack_rows(qq[i, pl.ds(3 * TOK_TILE, STAT_ROWS), :], 0)
        grads[i, :, pl.ds(0, HD)] = root_back(dq[...].T * ATT_SCALE, query_unit, factor)
        return carry

    lax.fori_loop(0, count, per_query, 0)

    def finish(j, carry):
        key_unit = kv[j, first, :].astype(jnp.float32) + qq[
            j, pl.ds(2 * TOK_TILE, TOK_TILE), :
        ].astype(jnp.float32)
        factor = unpack_rows(qq[j, pl.ds(3 * TOK_TILE, STAT_ROWS), :], 1)
        grads[j, :, pl.ds(HD, HD)] = root_back(dk[j] * ATT_SCALE, key_unit, factor)
        grads[j, :, pl.ds(2 * HD, HD)] = dv[j].astype(jnp.bfloat16)
        return carry

    lax.fori_loop(0, count, finish, 0)
    out_ref[...] = jnp.zeros_like(out_ref)

    def weight(j, carry):
        out_ref[...] += mm(nb[j], grads[j], TN)
        return carry

    lax.fori_loop(0, count, weight, 0)


def root_back(grad_unit, unit_value, factor_row):
    factor = jnp.broadcast_to(factor_row, (HD, TOK_TILE)).T
    inner = jnp.mean(grad_unit * unit_value, -1, keepdims=True)
    return (factor * (grad_unit - unit_value * inner)).astype(jnp.bfloat16)


def vmem():
    return pl.BlockSpec(memory_space=pltpu.VMEM)


def params():
    return pltpu.CompilerParams(vmem_limit_bytes=VMEM_BYTES)


def per_device(
    count, heads, tokens, mod_shift, mod_scale, mod_gate, qkv_weight, out_weight, teacher, slot_tiles
):
    features = tokens.shape[1]
    part = features // count
    quarter = TOK_TILE // heads
    width_tiles = count // (TT * TH)
    me = lax.axis_index("tile")
    my_head = lax.axis_index("head")
    source_table, target_table = ring_tables(count)
    source = jnp.asarray(source_table)[me]
    target = jnp.asarray(target_table)[me]
    onehot = (source[:, None] == jnp.arange(count, dtype=jnp.int32)[None, :]).astype(jnp.int32)
    rel_tiles = jnp.sum(onehot * slot_tiles[None, :], 1)
    allowed = near_tiles(rel_tiles, rel_tiles, width_tiles)

    out_weights = head_gather_doubling(out_weight, heads)

    bf16, f32 = jnp.bfloat16, jnp.float32
    normed, kv, qq = pl.pallas_call(
        project_kernel,
        out_shape=(
            jax.ShapeDtypeStruct((TOK_TILE, features), bf16),
            jax.ShapeDtypeStruct((2 * TOK_TILE, HD), bf16),
            jax.ShapeDtypeStruct((3 * TOK_TILE + STAT_ROWS, HD), bf16),
        ),
        in_specs=[vmem()] * 4,
        out_specs=(vmem(),) * 3,
        compiler_params=params(),
        name="project",
    )(tokens, mod_shift[None, :], mod_scale[None, :], qkv_weight)

    kv_all = ring_gather(kv, count)
    qq_all = ring_gather(qq, count)

    mine = lax.dynamic_slice_in_dim(normed, my_head * quarter, quarter, 0)
    slices = []
    for index, rel in enumerate(rel_offsets(count)):
        piece = lax.dynamic_slice_in_dim(mine, target[index] * part, part, 1)
        if rel:
            piece = lax.ppermute(piece, "tile", shift_perm(count, -rel))
        slices.append(piece)
    slab = jnp.stack(slices, 0)
    slabs = head_gather_doubling(slab, heads)
    normed_part = jnp.zeros((count, heads, quarter, part), bf16)
    for mask in range(heads):
        normed_part = lax.dynamic_update_slice(
            normed_part, slabs[mask][:, None], (0, my_head ^ mask, 0, 0)
        )
    normed_part = normed_part.reshape(count, TOK_TILE, part)

    attended, inverse = pl.pallas_call(
        functools.partial(attend_kernel, count),
        out_shape=(
            jax.ShapeDtypeStruct((TOK_TILE, HD), bf16),
            jax.ShapeDtypeStruct((1, TOK_TILE), f32),
        ),
        in_specs=[pl.BlockSpec(memory_space=pltpu.SMEM)] + [vmem()] * (1 + count),
        out_specs=(vmem(),) * 2,
        scratch_shapes=[
            pltpu.VMEM((count, TOK_TILE, TOK_TILE), f32),
            pltpu.VMEM((1, TOK_TILE), f32),
            pltpu.VMEM((HD, TOK_TILE), f32),
        ],
        compiler_params=params(),
        name="attend",
    )(allowed, qq, *kv_all)

    attended_all = head_gather_direct(attended, heads)

    chunk = 512
    row = pl.BlockSpec((1, chunk), lambda j: (0, j))
    whole_att = pl.BlockSpec((TOK_TILE, HD), lambda j: (0, 0))
    grad_att, out_term = pl.pallas_call(
        functools.partial(branch_kernel, heads),
        grid=(features // chunk,),
        out_shape=(
            jax.ShapeDtypeStruct((TOK_TILE + STAT_ROWS, HD), bf16),
            jax.ShapeDtypeStruct((HD, features), f32),
        ),
        in_specs=[
            pl.BlockSpec((1, TOK_TILE), lambda j: (0, 0)),
            row,
            pl.BlockSpec((TOK_TILE, chunk), lambda j: (0, j)),
        ]
        + [whole_att] * heads
        + [pl.BlockSpec((HD, chunk), lambda j: (0, j))] * heads,
        out_specs=(
            pl.BlockSpec((TOK_TILE + STAT_ROWS, HD), lambda j: (0, 0)),
            pl.BlockSpec((HD, chunk), lambda j: (0, j)),
        ),
        scratch_shapes=[pltpu.VMEM((TOK_TILE, HD), f32)],
        compiler_params=params(),
        name="branch",
    )(inverse, mod_gate[None, :], teacher, *attended_all, *out_weights)

    ga_all = ring_gather(grad_att, count)

    top = jnp.max(jnp.abs(out_term), 0, keepdims=True)
    power = jnp.floor(jnp.log2(jnp.clip(top, 2.0**-100, 2.0**100))) - 10.0
    scaled = jnp.concatenate(
        [out_term * jnp.exp2(-power), jnp.broadcast_to(power, (16, features))], 0
    ).astype(jnp.float16)
    out_grad = lax.dynamic_slice_in_dim(out_term, me * part, part, 1)
    for index, rel in enumerate(rel_offsets(count)):
        if rel:
            piece = lax.dynamic_slice_in_dim(scaled, target[index] * part, part, 1)
            piece = lax.ppermute(piece, "tile", shift_perm(count, -rel)).astype(f32)
            out_grad += piece[:HD] * jnp.exp2(piece[HD : HD + 1])

    hbm = pl.BlockSpec(memory_space=pl.ANY)
    qkv_grad = pl.pallas_call(
        functools.partial(backward_kernel, count),
        out_shape=jax.ShapeDtypeStruct((part, 3 * HD), f32),
        in_specs=[pl.BlockSpec(memory_space=pltpu.SMEM)] + [hbm] * (3 * count + 1),
        out_specs=vmem(),
        scratch_shapes=[
            pltpu.VMEM((count, 2 * TOK_TILE, HD), bf16),
            pltpu.VMEM((count, 3 * TOK_TILE + STAT_ROWS, HD), bf16),
            pltpu.VMEM((count, TOK_TILE + STAT_ROWS, HD), bf16),
            pltpu.VMEM((count, TOK_TILE, part), bf16),
            pltpu.VMEM((HD, TOK_TILE), f32),
            pltpu.VMEM((count, TOK_TILE, HD), f32),
            pltpu.VMEM((count, TOK_TILE, HD), f32),
            pltpu.VMEM((count, TOK_TILE, 3 * HD), bf16),
            pltpu.SemaphoreType.DMA((3 * count + 1,)),
        ],
        compiler_params=params(),
        name="backward",
    )(allowed, *kv_all, *qq_all, *ga_all, normed_part)
    return (qkv_grad, out_grad)


def solution(mesh):
    return jax.shard_map(
        functools.partial(per_device, mesh.shape["tile"], mesh.shape["head"]),
        mesh=mesh,
        in_specs=(
            P("tile", None),
            P(),
            P(),
            P(),
            P(None, "head"),
            P("head", None),
            P("tile", None),
            P(),
        ),
        out_specs=(P("tile", "head"), P("head", "tile")),
        check_vma=False,
    )
```

time: 506 us -> 208 us (0.41)
  waiting for transfers between devices: 376 us -> 71 us
  blocking collectives: 66.1 us -> 0 us
  starting transfers between devices: 0.39 us -> 57.2 us
  Pallas kernels: 0 us -> 53.7 us
  matrix products: 30.5 us -> 0 us
  local copies, waits for them, and re-layouts: 3.33 us -> 15.5 us
  between operations: 16.7 us -> 6.46 us
  other arithmetic: 12.2 us -> 3.97 us
    reduce_scatter x4 -> x0, waiting for transfers between devices: 281 us -> none  [the longest x1 99.2 us: per_device(): lax.psum_scatter(qkv_term, 'tile', scatter_dimension=0, tiled=True)]
    psum x1 -> x0, waiting for transfers between devices: 95.3 us -> none  [per_device(): whole_branch = lax.psum(partial_branch, 'head')]
    ppermute x0 -> x44, waiting for transfers between devices: none -> 71 us  [the longest x7 26.8 us: per_device(): piece = lax.ppermute(piece, 'tile', shift_perm(count, -rel)).astype(f32)]
    all_gather x2 -> x0, blocking collectives: 66.1 us -> none  [the longest x1 33.9 us: per_device(): lax.all_gather(key_b, 'tile', axis=0, tiled=True)]
    ppermute x0 -> x44, starting transfers between devices: none -> 57.2 us  [the longest x7 20.5 us: per_device(): piece = lax.ppermute(piece, 'tile', shift_perm(count, -rel))]
    pallas_call x0 -> x4, Pallas kernels: none -> 53.7 us  [the longest x1 34.2 us: per_device(): pl.pallas_call(functools.partial(backward_kernel, count), out_shape=jax.S...]
    dot_general x11 -> x0, matrix products: 30.5 us -> none  [the longest x1 5.59 us: per_device(): lax.dot_general(normed, grad_qkv, contract_rows, preferred_element_type=j...]
    reduce_sum x4 -> x1, other arithmetic: 5.97 us -> 0.18 us  [per_device(): rel_tiles = jnp.sum(onehot * slot_tiles[None, :], 1)]
  transfers between devices with their start and end apart: 5 -> 44, of which waited for: 5 -> 25; matrix products, arithmetic and copies ran while one was open for 4% -> 8% of each run, Pallas kernels for 0% -> 6%
where the time goes in v1:
time: 208 us
  waiting for transfers between devices  71 us (34%)
  starting transfers between devices  57.2 us (28%)
  Pallas kernels  53.7 us (26%)
  local copies, waits for them, and re-layouts  15.5 us (7%)
  between operations  6.46 us (3%)
  other arithmetic  3.97 us (2%)
    pallas_call x1, Pallas kernels, per_device(): pl.pallas_call(functools.partial(backward_kernel, count), out_shape=jax.S...  34.2 us
    ppermute x7, waiting for transfers between devices, per_device(): piece = lax.ppermute(piece, 'tile', shift_perm(count, -rel)).astype(f32)  26.8 us
    ppermute x7, starting transfers between devices, per_device(): piece = lax.ppermute(piece, 'tile', shift_perm(count, -rel))  20.5 us
    ppermute x12, waiting for transfers between devices, ring_gather(): up.append(lax.ppermute(up[-1], 'tile', shift_perm(count, 1)))  16.4 us
    ppermute x9, starting transfers between devices, ring_gather(): down.append(lax.ppermute(down[-1], 'tile', shift_perm(count, -1)))  15.3 us
    ppermute x7, waiting for transfers between devices, per_device(): piece = lax.ppermute(piece, 'tile', shift_perm(count, -rel))  15.2 us
    pallas_call x1, Pallas kernels, per_device(): pl.pallas_call(functools.partial(branch_kernel, heads), grid=(features //...  8.71 us
    ppermute x12, starting transfers between devices, ring_gather(): up.append(lax.ppermute(up[-1], 'tile', shift_perm(count, 1)))  8.69 us
  transfers between devices with their start and end apart: 44, of which 25 were waited for; matrix products, arithmetic and copies ran while one was open for 8% of the time, Pallas kernels for 6%

profile of v1, /device:TPU:0, one launch (start us, length us, event | category | flops | bytes accessed | tf_op | source)
XLA Modules:
  0.0 207.8 jit_solution(3221648163737903422)
XLA Ops:
  0.6 6.3 %project.1 = (bf16[384,3072]{1,0:T(8,128)(2,1)}, bf16[768,128]{1,0:T(8,128)(2,1)}, bf16[1184,128]{1,0:T(8,128)(2,1)}) custom-call(bf16[384,3072]{1,0:T(8,128)(2,1)} %tok_ref.1, f32[1,3072]{1,0:T(1,128)} %bitcast.47, f32[1,3072]{1,0:T(1,128)} %bitcast.48, bf16[3072,384]{1,0:T(8,128)(2,1)} %w_ref.1), custom_call_target="tpu_custom_call" | custom-call | tf_op jit(solution)/shard_map/project/pallas_call | solution.py:323
  6.9 3.0 %collective-permute-start = (bf16[768,128]{1,0:T(8,128)(2,1)}, bf16[768,128]{1,0:T(8,128)(2,1)S(1)}, u32[]{:S(2)}, u32[]{:S(2)}) collective-permute-start(bf16[768,128]{1,0:T(8,128)(2,1)} %get-tuple-element.9.refs_0_), channel_id=1, source_target_pairs={{0,8},{8,16},{16,24},{24,28},{28,20},{20,12},{12,4},{4,0},{1,9},{9... | collective-permute-start | bytes 589832 | tf_op jit(solution)/shard_map/ppermute | solution.py:66
  10.0 2.0 collective-permute-start.7
  12.0 0.7 constant_dynamic-slice_fusion
  12.7 0.7 fusion.35
  17.8 1.6 fusion.34
  19.4 2.1 collective-permute-start.27
  22.2 1.6 bitcast_dynamic-update-slice_fusion.11
  23.8 2.0 collective-permute-start.28
  25.8 0.6 bitcast_dynamic-update-slice_fusion.10
  26.4 1.7 collective-permute-done.28
  28.2 3.0 %collective-permute-start.29 = (bf16[96,384]{1,0:T(8,128)(2,1)S(1)}, bf16[96,384]{1,0:T(8,128)(2,1)S(1)}, u32[]{:S(2)}, u32[]{:S(2)}) collective-permute-start(bf16[96,384]{1,0:T(8,128)(2,1)S(1)} %get-tuple-element.20), channel_id=1, source_target_pairs={{0,16},{8,24},{16,28},{24,20},{28,12},{20,4},{12,0},{4,8},{1,17},{... | collective-permute-start | bytes 221192 | tf_op jit(solution)/shard_map/ppermute | solution.py:344
  31.2 0.6 bitcast_dynamic-update-slice_fusion.9
  31.9 2.0 collective-permute-done.29
  33.9 3.5 %collective-permute-start.30 = (bf16[96,384]{1,0:T(8,128)(2,1)S(1)}, bf16[96,384]{1,0:T(8,128)(2,1)S(1)}, u32[]{:S(2)}, u32[]{:S(2)}) collective-permute-start(bf16[96,384]{1,0:T(8,128)(2,1)S(1)} %get-tuple-element.19), channel_id=1, source_target_pairs={{0,12},{8,4},{16,0},{24,8},{28,16},{20,24},{12,28},{4,20},{1,13},{... | collective-permute-start | bytes 221192 | tf_op jit(solution)/shard_map/ppermute | solution.py:344
  37.4 0.6 bitcast_dynamic-update-slice_fusion.8
  38.0 1.7 collective-permute-done.30
  39.8 3.8 %collective-permute-start.31 = (bf16[96,384]{1,0:T(8,128)(2,1)S(1)}, bf16[96,384]{1,0:T(8,128)(2,1)S(1)}, u32[]{:S(2)}, u32[]{:S(2)}) collective-permute-start(bf16[96,384]{1,0:T(8,128)(2,1)S(1)} %get-tuple-element.18), channel_id=1, source_target_pairs={{0,24},{8,28},{16,20},{24,12},{28,4},{20,0},{12,8},{4,16},{1,25},{... | collective-permute-start | bytes 221192 | tf_op jit(solution)/shard_map/ppermute | solution.py:344
  43.6 0.6 bitcast_dynamic-update-slice_fusion.7
  44.2 2.5 %collective-permute-done.31 = bf16[96,384]{1,0:T(8,128)(2,1)S(1)} collective-permute-done((bf16[96,384]{1,0:T(8,128)(2,1)S(1)}, bf16[96,384]{1,0:T(8,128)(2,1)S(1)}, u32[]{:S(2)}, u32[]{:S(2)}) %collective-permute-start.31) | collective-permute-done | bytes 73760 | tf_op jit(solution)/shard_map/ppermute | solution.py:344
  46.7 1.1 collective-permute-start.32
  47.8 0.6 bitcast_dynamic-update-slice_fusion.6
  48.4 4.8 %collective-permute-done.32 = bf16[96,384]{1,0:T(8,128)(2,1)S(1)} collective-permute-done((bf16[96,384]{1,0:T(8,128)(2,1)S(1)}, bf16[96,384]{1,0:T(8,128)(2,1)S(1)}, u32[]{:S(2)}, u32[]{:S(2)}) %collective-permute-start.32) | collective-permute-done | bytes 73760 | tf_op jit(solution)/shard_map/ppermute | solution.py:344
  53.3 5.1 %collective-permute-start.33 = (bf16[96,384]{1,0:T(8,128)(2,1)S(1)}, bf16[96,384]{1,0:T(8,128)(2,1)S(1)}, u32[]{:S(2)}, u32[]{:S(2)}) collective-permute-start(bf16[96,384]{1,0:T(8,128)(2,1)S(1)} %get-tuple-element.16), channel_id=1, source_target_pairs={{0,28},{8,20},{16,12},{24,4},{28,0},{20,8},{12,16},{4,24},{1,29},{... | collective-permute-start | bytes 221192 | tf_op jit(solution)/shard_map/ppermute | solution.py:344
  59.0 2.4 %collective-permute-done.33 = bf16[96,384]{1,0:T(8,128)(2,1)S(1)} collective-permute-done((bf16[96,384]{1,0:T(8,128)(2,1)S(1)}, bf16[96,384]{1,0:T(8,128)(2,1)S(1)}, u32[]{:S(2)}, u32[]{:S(2)}) %collective-permute-start.33) | collective-permute-done | bytes 73760 | tf_op jit(solution)/shard_map/ppermute | solution.py:344
  61.3 1.5 collective-permute-start.18
  64.0 2.0 collective-permute-start.3
  66.0 0.7 fusion.33
  67.0 2.7 %collective-permute-done.2.refs_3_ = bf16[768,128]{1,0:T(8,128)(2,1)S(1)} collective-permute-done((bf16[768,128]{1,0:T(8,128)(2,1)S(1)}, bf16[768,128]{1,0:T(8,128)(2,1)S(1)}, u32[]{:S(2)}, u32[]{:S(2)}) %collective-permute-start.2) | collective-permute-done | bytes 196640 | tf_op jit(solution)/shard_map/ppermute | solution.py:66
  69.8 2.0 collective-permute-start.5
  71.8 3.6 %collective-permute-done.4.refs_5_ = bf16[768,128]{1,0:T(8,128)(2,1)S(1)} collective-permute-done((bf16[768,128]{1,0:T(8,128)(2,1)S(1)}, bf16[768,128]{1,0:T(8,128)(2,1)S(1)}, u32[]{:S(2)}, u32[]{:S(2)}) %collective-permute-start.4) | collective-permute-done | bytes 196640 | tf_op jit(solution)/shard_map/ppermute | solution.py:66
  75.4 1.6 collective-permute-start.9
  77.1 0.7 fusion.17.allowed_ref
  77.7 6.3 %collective-permute-done.35 = bf16[8,96,384]{2,1,0:T(8,128)(2,1)} collective-permute-done((bf16[8,96,384]{2,1,0:T(8,128)(2,1)}, bf16[8,96,384]{2,1,0:T(8,128)(2,1)}, u32[]{:S(2)}, u32[]{:S(2)}) %collective-permute-start.35) | collective-permute-done | bytes 589856 | tf_op jit(solution)/shard_map/ppermute | solution.py:84
  84.8 1.2 bitcast_dynamic-update-slice_fusion.3
  86.0 2.4 %collective-permute-start.10 = (bf16[1184,128]{1,0:T(8,128)(2,1)S(1)}, bf16[1184,128]{1,0:T(8,128)(2,1)S(1)}, u32[]{:S(2)}, u32[]{:S(2)}) collective-permute-start(bf16[1184,128]{1,0:T(8,128)(2,1)S(1)} %copy-done.15), channel_id=1, source_target_pairs={{0,4},{8,0},{16,8},{24,16},{28,24},{20,28},{12,20},{4,12},{1,5},{9... | collective-permute-start | bytes 909320 | tf_op jit(solution)/shard_map/ppermute | solution.py:68
  88.4 1.2 bitcast_dynamic-update-slice_fusion.2
  89.6 5.4 %collective-permute-done.6.refs_7_ = bf16[768,128]{1,0:T(8,128)(2,1)S(1)} collective-permute-done((bf16[768,128]{1,0:T(8,128)(2,1)S(1)}, bf16[768,128]{1,0:T(8,128)(2,1)S(1)}, u32[]{:S(2)}, u32[]{:S(2)}) %collective-permute-start.6) | collective-permute-done | bytes 196640 | tf_op jit(solution)/shard_map/ppermute | solution.py:66
  95.3 1.2 bitcast_dynamic-update-slice_fusion.1
  96.4 4.5 %attend.1 = (bf16[384,128]{1,0:T(8,128)(2,1)}, f32[1,384]{1,0:T(1,128)}) custom-call(s32[8,8]{1,0:T(8,128)} %fusion.17.allowed_ref, bf16[1184,128]{1,0:T(8,128)(2,1)} %get-tuple-element.10.q_ref.refs_8_, bf16[768,128]{1,0:T(8,128)(2,1)} %get-tuple-element.9.refs_0_, bf16[768,128]{1,0:T(8,128)(2,1)} %copy-done.6, bf16[768,128]{1,0:T(8,128)(2,1)} %copy-done.7, ...), custom_call_target="tpu_custom_call" | custom-call | tf_op jit(solution)/shard_map/attend/pallas_call | solution.py:355
  101.1 1.6 collective-permute-start.15
  103.1 2.9 %collective-permute-start.12 = (bf16[1184,128]{1,0:T(8,128)(2,1)S(1)}, bf16[1184,128]{1,0:T(8,128)(2,1)S(1)}, u32[]{:S(2)}, u32[]{:S(2)}) collective-permute-start(bf16[1184,128]{1,0:T(8,128)(2,1)S(1)} %collective-permute-done.10.refs_12_), channel_id=1, source_target_pairs={{0,4},{8,0},{16,8},{24,16},{28,24},{20,28},{12,20},{4,12},{1,5},{9... | collective-permute-start | bytes 909320 | tf_op jit(solution)/shard_map/ppermute | solution.py:68
  106.0 1.0 collective-permute-done.15.refs_2_
  107.0 1.2 collective-permute-done.16.refs_3_
  109.0 8.7 %branch.1 = (bf16[416,128]{1,0:T(8,128)(2,1)}, f32[128,3072]{1,0:T(8,128)}) custom-call(f32[1,384]{1,0:T(1,128)} %get-tuple-element.11.inv_ref, f32[1,3072]{1,0:T(1,128)} %bitcast.49, bf16[384,3072]{1,0:T(8,128)(2,1)} %teacher_ref.1, bf16[384,128]{1,0:T(8,128)(2,1)} %get-tuple-element.12.refs_0_, bf16[384,128]{1,0:T(8,128)(2,1)} %copy-done.28, ...), custom_call_target="tpu_custom_call" | custom-call | tf_op jit(solution)/shard_map/branch/pallas_call | solution.py:377
  117.8 1.6 abs_reduce_fusion
  120.0 3.7 %collective-permute-start.42 = (f16[144,384]{1,0:T(8,128)(2,1)S(1)}, f16[144,384]{1,0:T(8,128)(2,1)S(1)}, u32[]{:S(2)}, u32[]{:S(2)}) collective-permute-start(f16[144,384]{1,0:T(8,128)(2,1)S(1)} %get-tuple-element.28), channel_id=1, source_target_pairs={{0,20},{8,12},{16,4},{24,0},{28,8},{20,16},{12,24},{4,28},{1,21},{... | collective-permute-start | bytes 331784 | tf_op jit(solution)/shard_map/ppermute | solution.py:411
  123.7 1.7 collective-permute-start.41
  125.5 0.7 collective-permute-start.20
  126.2 3.1 %collective-permute-done.42 = f16[144,384]{1,0:T(8,128)(2,1)S(1)} collective-permute-done((f16[144,384]{1,0:T(8,128)(2,1)S(1)}, f16[144,384]{1,0:T(8,128)(2,1)S(1)}, u32[]{:S(2)}, u32[]{:S(2)}) %collective-permute-start.42) | collective-permute-done | bytes 110624 | tf_op jit(solution)/shard_map/ppermute | solution.py:411
  129.3 5.8 %collective-permute-start.21 = (bf16[416,128]{1,0:T(8,128)(2,1)S(1)}, bf16[416,128]{1,0:T(8,128)(2,1)S(1)}, u32[]{:S(2)}, u32[]{:S(2)}) collective-permute-start(bf16[416,128]{1,0:T(8,128)(2,1)S(1)} %copy-done.20), channel_id=1, source_target_pairs={{0,4},{8,0},{16,8},{24,16},{28,24},{20,28},{12,20},{4,12},{1,5},{9... | collective-permute-start | bytes 319496 | tf_op jit(solution)/shard_map/ppermute | solution.py:68
  135.2 7.6 %collective-permute-done.40 = f16[144,384]{1,0:T(8,128)(2,1)S(1)} collective-permute-done((f16[144,384]{1,0:T(8,128)(2,1)S(1)}, f16[144,384]{1,0:T(8,128)(2,1)S(1)}, u32[]{:S(2)}, u32[]{:S(2)}) %collective-permute-start.40) | collective-permute-done | bytes 110624 | tf_op jit(solution)/shard_map/ppermute | solution.py:411
  142.9 6.7 %collective-permute-done.39 = f16[144,384]{1,0:T(8,128)(2,1)S(1)} collective-permute-done((f16[144,384]{1,0:T(8,128)(2,1)S(1)}, f16[144,384]{1,0:T(8,128)(2,1)S(1)}, u32[]{:S(2)}, u32[]{:S(2)}) %collective-permute-start.39) | collective-permute-done | bytes 110624 | tf_op jit(solution)/shard_map/ppermute | solution.py:411
  149.9 4.4 %collective-permute-done.38 = f16[144,384]{1,0:T(8,128)(2,1)S(1)} collective-permute-done((f16[144,384]{1,0:T(8,128)(2,1)S(1)}, f16[144,384]{1,0:T(8,128)(2,1)S(1)}, u32[]{:S(2)}, u32[]{:S(2)}) %collective-permute-start.38) | collective-permute-done | bytes 110624 | tf_op jit(solution)/shard_map/ppermute | solution.py:411
  154.4 2.3 %collective-permute-start.43 = (f16[144,384]{1,0:T(8,128)(2,1)S(1)}, f16[144,384]{1,0:T(8,128)(2,1)S(1)}, u32[]{:S(2)}, u32[]{:S(2)}) collective-permute-start(f16[144,384]{1,0:T(8,128)(2,1)S(1)} %fusion.7), channel_id=1, source_target_pairs={{0,28},{8,20},{16,12},{24,4},{28,0},{20,8},{12,16},{4,24},{1,29},{... | collective-permute-start | bytes 331784 | tf_op jit(solution)/shard_map/ppermute | solution.py:411
  156.8 3.6 %collective-permute-done.37 = f16[144,384]{1,0:T(8,128)(2,1)S(1)} collective-permute-done((f16[144,384]{1,0:T(8,128)(2,1)S(1)}, f16[144,384]{1,0:T(8,128)(2,1)S(1)}, u32[]{:S(2)}, u32[]{:S(2)}) %collective-permute-start.37) | collective-permute-done | bytes 110624 | tf_op jit(solution)/shard_map/ppermute | solution.py:411
  160.7 1.4 collective-permute-done.43
  162.7 0.7 collective-permute-start.24
  163.5 2.5 %collective-permute-done.23.refs_20_ = bf16[416,128]{1,0:T(8,128)(2,1)S(1)} collective-permute-done((bf16[416,128]{1,0:T(8,128)(2,1)S(1)}, bf16[416,128]{1,0:T(8,128)(2,1)S(1)}, u32[]{:S(2)}, u32[]{:S(2)}) %collective-permute-start.23) | collective-permute-done | bytes 106528 | tf_op jit(solution)/shard_map/ppermute | solution.py:68
  166.0 2.1 collective-permute-done.24.refs_21_
  168.4 0.8 fusion
  169.2 1.5 collective-permute-done.25.refs_22_
  170.7 2.1 %collective-permute-done.26.refs_23_ = bf16[416,128]{1,0:T(8,128)(2,1)S(1)} collective-permute-done((bf16[416,128]{1,0:T(8,128)(2,1)S(1)}, bf16[416,128]{1,0:T(8,128)(2,1)S(1)}, u32[]{:S(2)}, u32[]{:S(2)}) %collective-permute-start.26) | collective-permute-done | bytes 106528 | tf_op jit(solution)/shard_map/ppermute | solution.py:66
  173.4 34.2 %backward.1 = f32[384,384]{1,0:T(8,128)} custom-call(s32[8,8]{1,0:T(8,128)} %fusion.17.allowed_ref, bf16[768,128]{1,0:T(8,128)(2,1)} %get-tuple-element.9.refs_0_, bf16[768,128]{1,0:T(8,128)(2,1)} %copy-done.6, bf16[768,128]{1,0:T(8,128)(2,1)} %copy-done.7, bf16[768,128]{1,0:T(8,128)(2,1)} %copy-done.8, bf16[768,128]{1,0:T(8,128)(2,1)} %copy-done.9, ...), custom_call_target="tpu_custom_call" | custom-call | tf_op jit(solution)/shard_map/backward/pallas_call | solution.py:415
  (133 shorter events, 7.8 us)
Async XLA Ops:
  0.6 60.7 %copy-start.2 = (bf16[128,3072]{1,0:T(8,128)(2,1)S(1)}, bf16[128,3072]{1,0:T(8,128)(2,1)}, u32[]{:S(2)}) copy-start(bf16[128,3072]{1,0:T(8,128)(2,1)} %refs_4_.1) | copy-start | bytes 2359300
  6.9 59.8 %copy-start.31 = (s32[8]{0:T(128)S(1)}, s32[8]{0:T(128)}, u32[]{:S(2)}) copy-start(s32[8]{0:T(128)} %param.17) | copy-start | bytes 100
  6.9 56.5 %collective-permute-start = (bf16[768,128]{1,0:T(8,128)(2,1)}, bf16[768,128]{1,0:T(8,128)(2,1)S(1)}, u32[]{:S(2)}, u32[]{:S(2)}) collective-permute-start(bf16[768,128]{1,0:T(8,128)(2,1)} %get-tuple-element.9.refs_0_), channel_id=1, source_target_pairs={{0,8},{8,16},{16,24},{24,28},{28,20},{20,12},{12,4},{4,0},{1,9},{9... | collective-permute-start | bytes 589832 | tf_op jit(solution)/shard_map/ppermute | solution.py:66
  10.0 54.0 %collective-permute-start.1 = (bf16[768,128]{1,0:T(8,128)(2,1)}, bf16[768,128]{1,0:T(8,128)(2,1)S(1)}, u32[]{:S(2)}, u32[]{:S(2)}) collective-permute-start(bf16[768,128]{1,0:T(8,128)(2,1)} %get-tuple-element.9.refs_0_), channel_id=1, source_target_pairs={{0,4},{8,0},{16,8},{24,16},{28,24},{20,28},{12,20},{4,12},{1,5},{9... | collective-permute-start | bytes 589832 | tf_op jit(solution)/shard_map/ppermute | solution.py:68
  10.0 54.1 %collective-permute-start.7 = (bf16[1184,128]{1,0:T(8,128)(2,1)}, bf16[1184,128]{1,0:T(8,128)(2,1)S(1)}, u32[]{:S(2)}, u32[]{:S(2)}) collective-permute-start(bf16[1184,128]{1,0:T(8,128)(2,1)} %get-tuple-element.10.q_ref.refs_8_), channel_id=1, source_target_pairs={{0,8},{8,16},{16,24},{24,28},{28,20},{20,12},{12,4},{4,0},{1,9},{9... | collective-permute-start | bytes 909320 | tf_op jit(solution)/shard_map/ppermute | solution.py:66
  12.0 54.9 %collective-permute-start.8 = (bf16[1184,128]{1,0:T(8,128)(2,1)}, bf16[1184,128]{1,0:T(8,128)(2,1)S(1)}, u32[]{:S(2)}, u32[]{:S(2)}) collective-permute-start(bf16[1184,128]{1,0:T(8,128)(2,1)} %get-tuple-element.10.q_ref.refs_8_), channel_id=1, source_target_pairs={{0,4},{8,0},{16,8},{24,16},{28,24},{20,28},{12,20},{4,12},{1,5},{9... | collective-permute-start | bytes 909320 | tf_op jit(solution)/shard_map/ppermute | solution.py:68
  19.4 4.4 %collective-permute-start.27 = (bf16[96,384]{1,0:T(8,128)(2,1)S(1)}, bf16[96,384]{1,0:T(8,128)(2,1)S(1)}, u32[]{:S(2)}, u32[]{:S(2)}) collective-permute-start(bf16[96,384]{1,0:T(8,128)(2,1)S(1)} %get-tuple-element.22), channel_id=1, source_target_pairs={{0,8},{8,16},{16,24},{24,28},{28,20},{20,12},{12,4},{4,0},{1,9},{9... | collective-permute-start | bytes 221192 | tf_op jit(solution)/shard_map/ppermute | solution.py:344
  23.8 4.4 %collective-permute-start.28 = (bf16[96,384]{1,0:T(8,128)(2,1)S(1)}, bf16[96,384]{1,0:T(8,128)(2,1)S(1)}, u32[]{:S(2)}, u32[]{:S(2)}) collective-permute-start(bf16[96,384]{1,0:T(8,128)(2,1)S(1)} %get-tuple-element.21), channel_id=1, source_target_pairs={{0,4},{8,0},{16,8},{24,16},{28,24},{20,28},{12,20},{4,12},{1,5},{9... | collective-permute-start | bytes 221192 | tf_op jit(solution)/shard_map/ppermute | solution.py:344
  28.2 5.7 %collective-permute-start.29 = (bf16[96,384]{1,0:T(8,128)(2,1)S(1)}, bf16[96,384]{1,0:T(8,128)(2,1)S(1)}, u32[]{:S(2)}, u32[]{:S(2)}) collective-permute-start(bf16[96,384]{1,0:T(8,128)(2,1)S(1)} %get-tuple-element.20), channel_id=1, source_target_pairs={{0,16},{8,24},{16,28},{24,20},{28,12},{20,4},{12,0},{4,8},{1,17},{... | collective-permute-start | bytes 221192 | tf_op jit(solution)/shard_map/ppermute | solution.py:344
  33.9 5.9 %collective-permute-start.30 = (bf16[96,384]{1,0:T(8,128)(2,1)S(1)}, bf16[96,384]{1,0:T(8,128)(2,1)S(1)}, u32[]{:S(2)}, u32[]{:S(2)}) collective-permute-start(bf16[96,384]{1,0:T(8,128)(2,1)S(1)} %get-tuple-element.19), channel_id=1, source_target_pairs={{0,12},{8,4},{16,0},{24,8},{28,16},{20,24},{12,28},{4,20},{1,13},{... | collective-permute-start | bytes 221192 | tf_op jit(solution)/shard_map/ppermute | solution.py:344
  39.8 7.0 %collective-permute-start.31 = (bf16[96,384]{1,0:T(8,128)(2,1)S(1)}, bf16[96,384]{1,0:T(8,128)(2,1)S(1)}, u32[]{:S(2)}, u32[]{:S(2)}) collective-permute-start(bf16[96,384]{1,0:T(8,128)(2,1)S(1)} %get-tuple-element.18), channel_id=1, source_target_pairs={{0,24},{8,28},{16,20},{24,12},{28,4},{20,0},{12,8},{4,16},{1,25},{... | collective-permute-start | bytes 221192 | tf_op jit(solution)/shard_map/ppermute | solution.py:344
  46.7 6.6 %collective-permute-start.32 = (bf16[96,384]{1,0:T(8,128)(2,1)S(1)}, bf16[96,384]{1,0:T(8,128)(2,1)S(1)}, u32[]{:S(2)}, u32[]{:S(2)}) collective-permute-start(bf16[96,384]{1,0:T(8,128)(2,1)S(1)} %get-tuple-element.17), channel_id=1, source_target_pairs={{0,20},{8,12},{16,4},{24,0},{28,8},{20,16},{12,24},{4,28},{1,21},{... | collective-permute-start | bytes 221192 | tf_op jit(solution)/shard_map/ppermute | solution.py:344
  53.3 8.1 %collective-permute-start.33 = (bf16[96,384]{1,0:T(8,128)(2,1)S(1)}, bf16[96,384]{1,0:T(8,128)(2,1)S(1)}, u32[]{:S(2)}, u32[]{:S(2)}) collective-permute-start(bf16[96,384]{1,0:T(8,128)(2,1)S(1)} %get-tuple-element.16), channel_id=1, source_target_pairs={{0,28},{8,20},{16,12},{24,4},{28,0},{20,8},{12,16},{4,24},{1,29},{... | collective-permute-start | bytes 221192 | tf_op jit(solution)/shard_map/ppermute | solution.py:344
  61.3 22.7 %collective-permute-start.18 = (bf16[128,3072]{1,0:T(8,128)(2,1)S(1)}, bf16[128,3072]{1,0:T(8,128)(2,1)S(1)}, u32[]{:S(2)}, u32[]{:S(2)}) collective-permute-start(bf16[128,3072]{1,0:T(8,128)(2,1)S(1)} %copy-done.2), channel_id=1, source_target_pairs={{0,2},{1,3},{2,0},{3,1},{4,6},{5,7},{6,4},{7,5},{8,10},{9,11},{10,... | collective-permute-start | bytes 2359304 | tf_op jit(solution)/shard_map/ppermute | solution.py:84
  63.5 26.1 %copy-start.6 = (bf16[768,128]{1,0:T(8,128)(2,1)}, bf16[768,128]{1,0:T(8,128)(2,1)S(1)}, u32[]{:S(2)}) copy-start(bf16[768,128]{1,0:T(8,128)(2,1)S(1)} %collective-permute-done.refs_1_) | copy-start | bytes 589828
  63.5 20.5 %collective-permute-start.35 = (bf16[8,96,384]{2,1,0:T(8,128)(2,1)}, bf16[8,96,384]{2,1,0:T(8,128)(2,1)}, u32[]{:S(2)}, u32[]{:S(2)}) collective-permute-start(bf16[8,96,384]{2,1,0:T(8,128)(2,1)} %bitcast_dynamic-update-slice_fusion.4), channel_id=1, source_target_pairs={{0,2},{1,3},{2,0},{3,1},{4,6},{5,7},{6,4},{7,5},{8,10},{9,11},{10,... | collective-permute-start | bytes 1769480 | tf_op jit(solution)/shard_map/ppermute | solution.py:84
  64.0 25.6 %copy-start.7 = (bf16[768,128]{1,0:T(8,128)(2,1)}, bf16[768,128]{1,0:T(8,128)(2,1)S(1)}, u32[]{:S(2)}) copy-start(bf16[768,128]{1,0:T(8,128)(2,1)S(1)} %collective-permute-done.1.refs_2_) | copy-start | bytes 589828
  64.0 5.7 %collective-permute-start.2 = (bf16[768,128]{1,0:T(8,128)(2,1)S(1)}, bf16[768,128]{1,0:T(8,128)(2,1)S(1)}, u32[]{:S(2)}, u32[]{:S(2)}) collective-permute-start(bf16[768,128]{1,0:T(8,128)(2,1)S(1)} %collective-permute-done.refs_1_), channel_id=1, source_target_pairs={{0,8},{8,16},{16,24},{24,28},{28,20},{20,12},{12,4},{4,0},{1,9},{9... | collective-permute-start | bytes 589832 | tf_op jit(solution)/shard_map/ppermute | solution.py:66
  64.0 7.7 %copy-start.13 = (bf16[1184,128]{1,0:T(8,128)(2,1)}, bf16[1184,128]{1,0:T(8,128)(2,1)S(1)}, u32[]{:S(2)}) copy-start(bf16[1184,128]{1,0:T(8,128)(2,1)S(1)} %collective-permute-done.7.refs_9_) | copy-start | bytes 909316
  64.0 5.7 %collective-permute-start.3 = (bf16[768,128]{1,0:T(8,128)(2,1)S(1)}, bf16[768,128]{1,0:T(8,128)(2,1)S(1)}, u32[]{:S(2)}, u32[]{:S(2)}) collective-permute-start(bf16[768,128]{1,0:T(8,128)(2,1)S(1)} %collective-permute-done.1.refs_2_), channel_id=1, source_target_pairs={{0,4},{8,0},{16,8},{24,16},{28,24},{20,28},{12,20},{4,12},{1,5},{9... | collective-permute-start | bytes 589832 | tf_op jit(solution)/shard_map/ppermute | solution.py:68
  66.9 21.4 %collective-permute-start.34 = (bf16[8,96,384]{2,1,0:T(8,128)(2,1)}, bf16[8,96,384]{2,1,0:T(8,128)(2,1)}, u32[]{:S(2)}, u32[]{:S(2)}) collective-permute-start(bf16[8,96,384]{2,1,0:T(8,128)(2,1)} %bitcast_dynamic-update-slice_fusion.4), channel_id=1, source_target_pairs={{0,1},{1,0},{2,3},{3,2},{4,5},{5,4},{6,7},{7,6},{8,9},{9,8},{10,11... | collective-permute-start | bytes 1769480 | tf_op jit(solution)/shard_map/ppermute | solution.py:84
  69.7 19.9 %copy-start.8 = (bf16[768,128]{1,0:T(8,128)(2,1)}, bf16[768,128]{1,0:T(8,128)(2,1)S(1)}, u32[]{:S(2)}) copy-start(bf16[768,128]{1,0:T(8,128)(2,1)S(1)} %collective-permute-done.2.refs_3_) | copy-start | bytes 589828
  69.7 5.7 %collective-permute-start.4 = (bf16[768,128]{1,0:T(8,128)(2,1)S(1)}, bf16[768,128]{1,0:T(8,128)(2,1)S(1)}, u32[]{:S(2)}, u32[]{:S(2)}) collective-permute-start(bf16[768,128]{1,0:T(8,128)(2,1)S(1)} %collective-permute-done.2.refs_3_), channel_id=1, source_target_pairs={{0,8},{8,16},{16,24},{24,28},{28,20},{20,12},{12,4},{4,0},{1,9},{9... | collective-permute-start | bytes 589832 | tf_op jit(solution)/shard_map/ppermute | solution.py:66
  69.8 19.8 %copy-start.9 = (bf16[768,128]{1,0:T(8,128)(2,1)}, bf16[768,128]{1,0:T(8,128)(2,1)S(1)}, u32[]{:S(2)}) copy-start(bf16[768,128]{1,0:T(8,128)(2,1)S(1)} %collective-permute-done.3.refs_4_) | copy-start | bytes 589828
  69.8 5.7 %collective-permute-start.5 = (bf16[768,128]{1,0:T(8,128)(2,1)S(1)}, bf16[768,128]{1,0:T(8,128)(2,1)S(1)}, u32[]{:S(2)}, u32[]{:S(2)}) collective-permute-start(bf16[768,128]{1,0:T(8,128)(2,1)S(1)} %collective-permute-done.3.refs_4_), channel_id=1, source_target_pairs={{0,4},{8,0},{16,8},{24,16},{28,24},{20,28},{12,20},{4,12},{1,5},{9... | collective-permute-start | bytes 589832 | tf_op jit(solution)/shard_map/ppermute | solution.py:68
  75.4 14.2 %copy-start.10 = (bf16[768,128]{1,0:T(8,128)(2,1)}, bf16[768,128]{1,0:T(8,128)(2,1)S(1)}, u32[]{:S(2)}) copy-start(bf16[768,128]{1,0:T(8,128)(2,1)S(1)} %collective-permute-done.4.refs_5_) | copy-start | bytes 589828
  75.4 25.7 %collective-permute-start.17 = (bf16[128,3072]{1,0:T(8,128)(2,1)S(1)}, bf16[128,3072]{1,0:T(8,128)(2,1)S(1)}, u32[]{:S(2)}, u32[]{:S(2)}) collective-permute-start(bf16[128,3072]{1,0:T(8,128)(2,1)S(1)} %copy-done.2), channel_id=1, source_target_pairs={{0,1},{1,0},{2,3},{3,2},{4,5},{5,4},{6,7},{7,6},{8,9},{9,8},{10,11... | collective-permute-start | bytes 2359304 | tf_op jit(solution)/shard_map/ppermute | solution.py:84
  75.4 14.2 %copy-start.11 = (bf16[768,128]{1,0:T(8,128)(2,1)}, bf16[768,128]{1,0:T(8,128)(2,1)S(1)}, u32[]{:S(2)}) copy-start(bf16[768,128]{1,0:T(8,128)(2,1)S(1)} %collective-permute-done.5.refs_6_) | copy-start | bytes 589828
  75.4 10.5 %collective-permute-start.9 = (bf16[1184,128]{1,0:T(8,128)(2,1)}, bf16[1184,128]{1,0:T(8,128)(2,1)}, u32[]{:S(2)}, u32[]{:S(2)}) collective-permute-start(bf16[1184,128]{1,0:T(8,128)(2,1)} %copy-done.13), channel_id=1, source_target_pairs={{0,8},{8,16},{16,24},{24,28},{28,20},{20,12},{12,4},{4,0},{1,9},{9... | collective-permute-start | bytes 909320 | tf_op jit(solution)/shard_map/ppermute | solution.py:66
  77.7 8.3 %copy-start.15 = (bf16[1184,128]{1,0:T(8,128)(2,1)S(1)}, bf16[1184,128]{1,0:T(8,128)(2,1)}, u32[]{:S(2)}) copy-start(bf16[1184,128]{1,0:T(8,128)(2,1)} %copy-done.14) | copy-start | bytes 909316
  84.0 18.6 %collective-permute-start.36 = (bf16[8,96,384]{2,1,0:T(8,128)(2,1)}, bf16[8,96,384]{2,1,0:T(8,128)(2,1)S(1)}, u32[]{:S(2)}, u32[]{:S(2)}) collective-permute-start(bf16[8,96,384]{2,1,0:T(8,128)(2,1)} %collective-permute-done.35), channel_id=1, source_target_pairs={{0,1},{1,0},{2,3},{3,2},{4,5},{5,4},{6,7},{7,6},{8,9},{9,8},{10,11... | collective-permute-start | bytes 1769480 | tf_op jit(solution)/shard_map/ppermute | solution.py:84
  84.0 5.6 %copy-start.3 = (bf16[128,3072]{1,0:T(8,128)(2,1)}, bf16[128,3072]{1,0:T(8,128)(2,1)S(1)}, u32[]{:S(2)}) copy-start(bf16[128,3072]{1,0:T(8,128)(2,1)S(1)} %collective-permute-done.18.refs_6_) | copy-start | bytes 2359300
  84.0 24.1 %collective-permute-start.19 = (bf16[128,3072]{1,0:T(8,128)(2,1)S(1)}, bf16[128,3072]{1,0:T(8,128)(2,1)S(1)}, u32[]{:S(2)}, u32[]{:S(2)}) collective-permute-start(bf16[128,3072]{1,0:T(8,128)(2,1)S(1)} %collective-permute-done.18.refs_6_), channel_id=1, source_target_pairs={{0,1},{1,0},{2,3},{3,2},{4,5},{5,4},{6,7},{7,6},{8,9},{9,8},{10,11... | collective-permute-start | bytes 2359304 | tf_op jit(solution)/shard_map/ppermute | solution.py:84
  86.0 15.0 %collective-permute-start.10 = (bf16[1184,128]{1,0:T(8,128)(2,1)S(1)}, bf16[1184,128]{1,0:T(8,128)(2,1)S(1)}, u32[]{:S(2)}, u32[]{:S(2)}) collective-permute-start(bf16[1184,128]{1,0:T(8,128)(2,1)S(1)} %copy-done.15), channel_id=1, source_target_pairs={{0,4},{8,0},{16,8},{24,16},{28,24},{20,28},{12,20},{4,12},{1,5},{9... | collective-permute-start | bytes 909320 | tf_op jit(solution)/shard_map/ppermute | solution.py:68
  88.4 6.6 %collective-permute-start.6 = (bf16[768,128]{1,0:T(8,128)(2,1)S(1)}, bf16[768,128]{1,0:T(8,128)(2,1)S(1)}, u32[]{:S(2)}, u32[]{:S(2)}) collective-permute-start(bf16[768,128]{1,0:T(8,128)(2,1)S(1)} %collective-permute-done.4.refs_5_), channel_id=1, source_target_pairs={{0,8},{8,16},{16,24},{24,28},{28,20},{20,12},{12,4},{4,0},{1,9},{9... | collective-permute-start | bytes 589832 | tf_op jit(solution)/shard_map/ppermute | solution.py:66
  95.0 11.0 %collective-permute-start.11 = (bf16[1184,128]{1,0:T(8,128)(2,1)}, bf16[1184,128]{1,0:T(8,128)(2,1)S(1)}, u32[]{:S(2)}, u32[]{:S(2)}) collective-permute-start(bf16[1184,128]{1,0:T(8,128)(2,1)} %collective-permute-done.9.refs_11_), channel_id=1, source_target_pairs={{0,8},{8,16},{16,24},{24,28},{28,20},{20,12},{12,4},{4,0},{1,9},{9... | collective-permute-start | bytes 909320 | tf_op jit(solution)/shard_map/ppermute | solution.py:66
  101.0 16.8 %copy-start.16 = (bf16[1184,128]{1,0:T(8,128)(2,1)}, bf16[1184,128]{1,0:T(8,128)(2,1)S(1)}, u32[]{:S(2)}) copy-start(bf16[1184,128]{1,0:T(8,128)(2,1)S(1)} %collective-permute-done.10.refs_12_) | copy-start | bytes 909316
  101.0 2.1 collective-permute-start.14
  101.1 7.1 %copy-start.4 = (bf16[128,3072]{1,0:T(8,128)(2,1)}, bf16[128,3072]{1,0:T(8,128)(2,1)S(1)}, u32[]{:S(2)}) copy-start(bf16[128,3072]{1,0:T(8,128)(2,1)S(1)} %collective-permute-done.17.refs_5_) | copy-start | bytes 2359300
  101.1 5.9 %collective-permute-start.15 = (bf16[384,128]{1,0:T(8,128)(2,1)}, bf16[384,128]{1,0:T(8,128)(2,1)S(1)}, u32[]{:S(2)}, u32[]{:S(2)}) collective-permute-start(bf16[384,128]{1,0:T(8,128)(2,1)} %get-tuple-element.12.refs_0_), channel_id=1, source_target_pairs={{0,2},{1,3},{2,0},{3,1},{4,6},{5,7},{6,4},{7,5},{8,10},{9,11},{10,... | collective-permute-start | bytes 294920 | tf_op jit(solution)/shard_map/ppermute | solution.py:92
  102.6 5.5 %collective-permute-start.16 = (bf16[384,128]{1,0:T(8,128)(2,1)}, bf16[384,128]{1,0:T(8,128)(2,1)S(1)}, u32[]{:S(2)}, u32[]{:S(2)}) collective-permute-start(bf16[384,128]{1,0:T(8,128)(2,1)} %get-tuple-element.12.refs_0_), channel_id=1, source_target_pairs={{0,3},{1,2},{2,1},{3,0},{4,7},{5,6},{6,5},{7,4},{8,11},{9,10},{10,... | collective-permute-start | bytes 294920 | tf_op jit(solution)/shard_map/ppermute | solution.py:92
  103.0 14.7 %copy-start = (bf16[8,4,96,384]{3,2,1,0:T(8,128)(2,1)}, bf16[8,4,96,384]{3,2,1,0:T(8,128)(2,1)S(1)}, u32[]{:S(2)}) copy-start(bf16[8,4,96,384]{3,2,1,0:T(8,128)(2,1)S(1)} %bitcast_dynamic-update-slice_fusion) | copy-start | bytes 7077892
  103.1 66.1 %collective-permute-start.12 = (bf16[1184,128]{1,0:T(8,128)(2,1)S(1)}, bf16[1184,128]{1,0:T(8,128)(2,1)S(1)}, u32[]{:S(2)}, u32[]{:S(2)}) collective-permute-start(bf16[1184,128]{1,0:T(8,128)(2,1)S(1)} %collective-permute-done.10.refs_12_), channel_id=1, source_target_pairs={{0,4},{8,0},{16,8},{24,16},{28,24},{20,28},{12,20},{4,12},{1,5},{9... | collective-permute-start | bytes 909320 | tf_op jit(solution)/shard_map/ppermute | solution.py:68
  106.0 48.4 %copy-start.17 = (bf16[1184,128]{1,0:T(8,128)(2,1)}, bf16[1184,128]{1,0:T(8,128)(2,1)S(1)}, u32[]{:S(2)}) copy-start(bf16[1184,128]{1,0:T(8,128)(2,1)S(1)} %collective-permute-done.11.refs_13_) | copy-start | bytes 909316
  106.0 63.2 %collective-permute-start.13 = (bf16[1184,128]{1,0:T(8,128)(2,1)S(1)}, bf16[1184,128]{1,0:T(8,128)(2,1)S(1)}, u32[]{:S(2)}, u32[]{:S(2)}) collective-permute-start(bf16[1184,128]{1,0:T(8,128)(2,1)S(1)} %collective-permute-done.11.refs_13_), channel_id=1, source_target_pairs={{0,8},{8,16},{16,24},{24,28},{28,20},{20,12},{12,4},{4,0},{1,9},{9... | collective-permute-start | bytes 909320 | tf_op jit(solution)/shard_map/ppermute | solution.py:66
  119.4 6.1 %copy-start.20 = (bf16[416,128]{1,0:T(8,128)(2,1)S(1)}, bf16[416,128]{1,0:T(8,128)(2,1)}, u32[]{:S(2)}) copy-start(bf16[416,128]{1,0:T(8,128)(2,1)} %get-tuple-element.13.refs_16_) | copy-start | bytes 319492
  120.0 9.3 %collective-permute-start.42 = (f16[144,384]{1,0:T(8,128)(2,1)S(1)}, f16[144,384]{1,0:T(8,128)(2,1)S(1)}, u32[]{:S(2)}, u32[]{:S(2)}) collective-permute-start(f16[144,384]{1,0:T(8,128)(2,1)S(1)} %get-tuple-element.28), channel_id=1, source_target_pairs={{0,20},{8,12},{16,4},{24,0},{28,8},{20,16},{12,24},{4,28},{1,21},{... | collective-permute-start | bytes 331784 | tf_op jit(solution)/shard_map/ppermute | solution.py:411
  123.7 11.4 %collective-permute-start.41 = (f16[144,384]{1,0:T(8,128)(2,1)S(1)}, f16[144,384]{1,0:T(8,128)(2,1)S(1)}, u32[]{:S(2)}, u32[]{:S(2)}) collective-permute-start(f16[144,384]{1,0:T(8,128)(2,1)S(1)} %get-tuple-element.27), channel_id=1, source_target_pairs={{0,24},{8,28},{16,20},{24,12},{28,4},{20,0},{12,8},{4,16},{1,25},{... | collective-permute-start | bytes 331784 | tf_op jit(solution)/shard_map/ppermute | solution.py:411
  125.5 28.9 %collective-permute-start.20 = (bf16[416,128]{1,0:T(8,128)(2,1)S(1)}, bf16[416,128]{1,0:T(8,128)(2,1)S(1)}, u32[]{:S(2)}, u32[]{:S(2)}) collective-permute-start(bf16[416,128]{1,0:T(8,128)(2,1)S(1)} %copy-done.20), channel_id=1, source_target_pairs={{0,8},{8,16},{16,24},{24,28},{28,20},{20,12},{12,4},{4,0},{1,9},{9... | collective-permute-start | bytes 319496 | tf_op jit(solution)/shard_map/ppermute | solution.py:66
  129.3 27.4 %collective-permute-start.21 = (bf16[416,128]{1,0:T(8,128)(2,1)S(1)}, bf16[416,128]{1,0:T(8,128)(2,1)S(1)}, u32[]{:S(2)}, u32[]{:S(2)}) collective-permute-start(bf16[416,128]{1,0:T(8,128)(2,1)S(1)} %copy-done.20), channel_id=1, source_target_pairs={{0,4},{8,0},{16,8},{24,16},{28,24},{20,28},{12,20},{4,12},{1,5},{9... | collective-permute-start | bytes 319496 | tf_op jit(solution)/shard_map/ppermute | solution.py:68
  135.1 7.7 %collective-permute-start.40 = (f16[144,384]{1,0:T(8,128)(2,1)S(1)}, f16[144,384]{1,0:T(8,128)(2,1)S(1)}, u32[]{:S(2)}, u32[]{:S(2)}) collective-permute-start(f16[144,384]{1,0:T(8,128)(2,1)S(1)} %get-tuple-element.26), channel_id=1, source_target_pairs={{0,12},{8,4},{16,0},{24,8},{28,16},{20,24},{12,28},{4,20},{1,13},{... | collective-permute-start | bytes 331784 | tf_op jit(solution)/shard_map/ppermute | solution.py:411
  142.8 6.7 %collective-permute-start.39 = (f16[144,384]{1,0:T(8,128)(2,1)S(1)}, f16[144,384]{1,0:T(8,128)(2,1)S(1)}, u32[]{:S(2)}, u32[]{:S(2)}) collective-permute-start(f16[144,384]{1,0:T(8,128)(2,1)S(1)} %get-tuple-element.25), channel_id=1, source_target_pairs={{0,16},{8,24},{16,28},{24,20},{28,12},{20,4},{12,0},{4,8},{1,17},{... | collective-permute-start | bytes 331784 | tf_op jit(solution)/shard_map/ppermute | solution.py:411
  149.6 4.7 %collective-permute-start.38 = (f16[144,384]{1,0:T(8,128)(2,1)S(1)}, f16[144,384]{1,0:T(8,128)(2,1)S(1)}, u32[]{:S(2)}, u32[]{:S(2)}) collective-permute-start(f16[144,384]{1,0:T(8,128)(2,1)S(1)} %get-tuple-element.24), channel_id=1, source_target_pairs={{0,4},{8,0},{16,8},{24,16},{28,24},{20,28},{12,20},{4,12},{1,5},{9... | collective-permute-start | bytes 331784 | tf_op jit(solution)/shard_map/ppermute | solution.py:411
  154.3 6.1 %collective-permute-start.37 = (f16[144,384]{1,0:T(8,128)(2,1)S(1)}, f16[144,384]{1,0:T(8,128)(2,1)S(1)}, u32[]{:S(2)}, u32[]{:S(2)}) collective-permute-start(f16[144,384]{1,0:T(8,128)(2,1)S(1)} %get-tuple-element.23), channel_id=1, source_target_pairs={{0,8},{8,16},{16,24},{24,28},{28,20},{20,12},{12,4},{4,0},{1,9},{9... | collective-permute-start | bytes 331784 | tf_op jit(solution)/shard_map/ppermute | solution.py:411
  154.4 18.4 %copy-start.21 = (bf16[416,128]{1,0:T(8,128)(2,1)}, bf16[416,128]{1,0:T(8,128)(2,1)S(1)}, u32[]{:S(2)}) copy-start(bf16[416,128]{1,0:T(8,128)(2,1)S(1)} %collective-permute-done.20.refs_17_) | copy-start | bytes 319492
  154.4 7.7 %collective-permute-start.43 = (f16[144,384]{1,0:T(8,128)(2,1)S(1)}, f16[144,384]{1,0:T(8,128)(2,1)S(1)}, u32[]{:S(2)}, u32[]{:S(2)}) collective-permute-start(f16[144,384]{1,0:T(8,128)(2,1)S(1)} %fusion.7), channel_id=1, source_target_pairs={{0,28},{8,20},{16,12},{24,4},{28,0},{20,8},{12,16},{4,24},{1,29},{... | collective-permute-start | bytes 331784 | tf_op jit(solution)/shard_map/ppermute | solution.py:411
  156.7 16.0 %copy-start.22 = (bf16[416,128]{1,0:T(8,128)(2,1)}, bf16[416,128]{1,0:T(8,128)(2,1)S(1)}, u32[]{:S(2)}) copy-start(bf16[416,128]{1,0:T(8,128)(2,1)S(1)} %collective-permute-done.21.refs_18_) | copy-start | bytes 319492
  156.8 6.0 %collective-permute-start.22 = (bf16[416,128]{1,0:T(8,128)(2,1)S(1)}, bf16[416,128]{1,0:T(8,128)(2,1)S(1)}, u32[]{:S(2)}, u32[]{:S(2)}) collective-permute-start(bf16[416,128]{1,0:T(8,128)(2,1)S(1)} %collective-permute-done.20.refs_17_), channel_id=1, source_target_pairs={{0,8},{8,16},{16,24},{24,28},{28,20},{20,12},{12,4},{4,0},{1,9},{9... | collective-permute-start | bytes 319496 | tf_op jit(solution)/shard_map/ppermute | solution.py:66
  160.4 5.6 %collective-permute-start.23 = (bf16[416,128]{1,0:T(8,128)(2,1)S(1)}, bf16[416,128]{1,0:T(8,128)(2,1)S(1)}, u32[]{:S(2)}, u32[]{:S(2)}) collective-permute-start(bf16[416,128]{1,0:T(8,128)(2,1)S(1)} %collective-permute-done.21.refs_18_), channel_id=1, source_target_pairs={{0,4},{8,0},{16,8},{24,16},{28,24},{20,28},{12,20},{4,12},{1,5},{9... | collective-permute-start | bytes 319496 | tf_op jit(solution)/shard_map/ppermute | solution.py:68
  162.7 10.1 %copy-start.23 = (bf16[416,128]{1,0:T(8,128)(2,1)}, bf16[416,128]{1,0:T(8,128)(2,1)S(1)}, u32[]{:S(2)}) copy-start(bf16[416,128]{1,0:T(8,128)(2,1)S(1)} %collective-permute-done.22.refs_19_) | copy-start | bytes 319492
  162.7 5.3 %collective-permute-start.24 = (bf16[416,128]{1,0:T(8,128)(2,1)S(1)}, bf16[416,128]{1,0:T(8,128)(2,1)S(1)}, u32[]{:S(2)}, u32[]{:S(2)}) collective-permute-start(bf16[416,128]{1,0:T(8,128)(2,1)S(1)} %collective-permute-done.22.refs_19_), channel_id=1, source_target_pairs={{0,8},{8,16},{16,24},{24,28},{28,20},{20,12},{12,4},{4,0},{1,9},{9... | collective-permute-start | bytes 319496 | tf_op jit(solution)/shard_map/ppermute | solution.py:66
  166.0 6.8 %copy-start.24 = (bf16[416,128]{1,0:T(8,128)(2,1)}, bf16[416,128]{1,0:T(8,128)(2,1)S(1)}, u32[]{:S(2)}) copy-start(bf16[416,128]{1,0:T(8,128)(2,1)S(1)} %collective-permute-done.23.refs_20_) | copy-start | bytes 319492
  166.0 4.7 %collective-permute-start.25 = (bf16[416,128]{1,0:T(8,128)(2,1)S(1)}, bf16[416,128]{1,0:T(8,128)(2,1)S(1)}, u32[]{:S(2)}, u32[]{:S(2)}) collective-permute-start(bf16[416,128]{1,0:T(8,128)(2,1)S(1)} %collective-permute-done.23.refs_20_), channel_id=1, source_target_pairs={{0,4},{8,0},{16,8},{24,16},{28,24},{20,28},{12,20},{4,12},{1,5},{9... | collective-permute-start | bytes 319496 | tf_op jit(solution)/shard_map/ppermute | solution.py:68
  168.1 4.7 %collective-permute-start.26 = (bf16[416,128]{1,0:T(8,128)(2,1)S(1)}, bf16[416,128]{1,0:T(8,128)(2,1)S(1)}, u32[]{:S(2)}, u32[]{:S(2)}) collective-permute-start(bf16[416,128]{1,0:T(8,128)(2,1)S(1)} %collective-permute-done.24.refs_21_), channel_id=1, source_target_pairs={{0,8},{8,16},{16,24},{24,28},{28,20},{20,12},{12,4},{4,0},{1,9},{9... | collective-permute-start | bytes 319496 | tf_op jit(solution)/shard_map/ppermute | solution.py:66
  (12 other events, 30.8 us)

commit v2 on v1

--- a/solution.py
+++ b/solution.py
@@ -31,65 +31,6 @@
 
 def mm(a, b, dims):
     return lax.dot_general(a, b, dims, preferred_element_type=jnp.float32)
-
-
-def ring_order(count):
-    return [*range(0, count, 2), *range(count - 1 - (count % 2), 0, -2)]
-
-
-def rel_offsets(count):
-    offsets = [0]
-    for step in range(1, count // 2 + 1):
-        offsets.append(-step)
-        if len(offsets) < count:
-            offsets.append(step)
-    return offsets[:count]
-
-
-def ring_tables(count):
-    order = ring_order(count)
-    pos = [order.index(slot) for slot in range(count)]
-    rels = rel_offsets(count)
-    source = [[order[(pos[s] + rel) % count] for rel in rels] for s in range(count)]
-    target = [[order[(pos[s] - rel) % count] for rel in rels] for s in range(count)]
-    return np.array(source, np.int32), np.array(target, np.int32)
-
-
-def shift_perm(count, offset):
-    order = ring_order(count)
-    return [(order[p], order[(p + offset) % count]) for p in range(count)]
-
-
-def ring_gather(block, count):
-    up, down = [block], [block]
-    for _ in range(count // 2):
-        up.append(lax.ppermute(up[-1], "tile", shift_perm(count, 1)))
-    for _ in range((count - 1) // 2):
-        down.append(lax.ppermute(down[-1], "tile", shift_perm(count, -1)))
-    out = []
-    for rel in rel_offsets(count):
-        out.append(up[-rel] if rel <= 0 else down[rel])
-    return out
-
-
-def xor_perm(count, mask):
-    return [(h, h ^ mask) for h in range(count)]
-
-
-def head_gather_doubling(block, count):
-    blocks = [block]
-    mask = count // 2
-    masks = [0]
-    while mask:
-        moved = [lax.ppermute(b, "head", xor_perm(count, mask)) for b in blocks]
-        blocks = blocks + moved
-        masks = masks + [m ^ mask for m in masks]
-        mask //= 2
-    return [blocks[masks.index(m)] for m in range(count)]
-
-
-def head_gather_direct(block, count):
-    return [block] + [lax.ppermute(block, "head", xor_perm(count, m)) for m in range(1, count)]
 
 
 def near_tiles(first_tiles, second_tiles, width_tiles):
@@ -160,9 +101,7 @@
     q_ref[pl.ds(3 * TOK_TILE, STAT_ROWS), :] = pack_rows(query_rows + key_rows)
 
 
-def attend_kernel(count, allowed_ref, q_ref, *refs):
-    kv_refs = refs[:count]
-    att_ref, inv_ref, expo, totals, acc = refs[count:]
+def attend_kernel(count, allowed_ref, q_ref, kv_ref, att_ref, inv_ref, expo, totals, acc):
     query = q_ref[pl.ds(0, TOK_TILE), :]
     totals[...] = jnp.zeros_like(totals)
     acc[...] = jnp.zeros_like(acc)
@@ -170,7 +109,7 @@
 
         @pl.when(allowed_ref[0, r] != 0)
         def _():
-            scores = mm(kv_refs[r][pl.ds(0, TOK_TILE), :], query, NT)
+            scores = mm(kv_ref[r, pl.ds(0, TOK_TILE), :], query, NT)
             part = jnp.exp2(scores * EXP_SCALE)
             expo[r] = part
             totals[...] += jnp.sum(part, 0, keepdims=True)
@@ -182,58 +121,42 @@
         @pl.when(allowed_ref[0, r] != 0)
         def _():
             probs = (expo[r] * inverse).astype(jnp.bfloat16)
-            acc[...] += mm(kv_refs[r][pl.ds(TOK_TILE, TOK_TILE), :], probs, TN)
+            acc[...] += mm(kv_ref[r, pl.ds(TOK_TILE, TOK_TILE), :], probs, TN)
 
     att_ref[...] = acc[...].T.astype(jnp.bfloat16)
 
 
 def branch_kernel(heads, inv_ref, gate_ref, teacher_ref, *refs):
-    att_refs = refs[:heads]
-    w_refs = refs[heads : 2 * heads]
-    ga_ref, out_ref, acc = refs[2 * heads :]
+    own_att, own_w, all_att, all_w, ga_ref, out_ref, acc = refs
     step = pl.program_id(0)
 
     @pl.when(step == 0)
     def _():
         acc[...] = jnp.zeros_like(acc)
 
-    branch = mm(att_refs[0][...], w_refs[0][...], NN)
+    branch = mm(all_att[0], all_w[0], NN)
     for h in range(1, heads):
-        branch += mm(att_refs[h][...], w_refs[h][...], NN)
+        branch += mm(all_att[h], all_w[h], NN)
     gate = gate_ref[...]
     residual = LOSS_WEIGHT * (gate * branch - teacher_ref[...].astype(jnp.float32))
     grad = (gate * residual).astype(jnp.bfloat16)
-    out_ref[...] = mm(att_refs[0][...], grad, TN)
-    acc[...] += mm(grad, w_refs[0][...], NT)
+    out_ref[...] = mm(own_att[...], grad, TN)
+    acc[...] += mm(grad, own_w[...], NT)
 
     @pl.when(step == pl.num_programs(0) - 1)
     def _():
         grad_att = acc[...].astype(jnp.bfloat16)
         ga_ref[pl.ds(0, TOK_TILE), :] = grad_att
-        product = grad_att.astype(jnp.float32) * att_refs[0][...].astype(jnp.float32)
+        product = grad_att.astype(jnp.float32) * own_att[...].astype(jnp.float32)
         delta = jnp.sum(product.T, 0, keepdims=True)
         ga_ref[pl.ds(TOK_TILE, STAT_ROWS), :] = pack_rows(
             lane_chunks(inv_ref[...]) + lane_chunks(delta)
         )
 
 
-def backward_kernel(count, allowed_ref, *refs):
-    kv_in, q_in, ga_in = refs[:count], refs[count : 2 * count], refs[2 * count : 3 * count]
-    nb_in = refs[3 * count]
-    out_ref = refs[3 * count + 1]
-    kv, qq, ga, nb, dq, dk, dv, grads, sems = refs[3 * count + 2 :]
-    copies = []
-    for r in range(count):
-        copies.append(pltpu.make_async_copy(kv_in[r], kv.at[r], sems.at[3 * r]))
-        copies.append(pltpu.make_async_copy(q_in[r], qq.at[r], sems.at[3 * r + 1]))
-        copies.append(pltpu.make_async_copy(ga_in[r], ga.at[r], sems.at[3 * r + 2]))
-    copies.append(pltpu.make_async_copy(nb_in, nb, sems.at[3 * count]))
-    for copy in copies:
-        copy.start()
+def backward_kernel(count, allowed_ref, kv, qq, ga, nb, out_ref, dq, dk, dv, grads):
     dk[...] = jnp.zeros_like(dk)
     dv[...] = jnp.zeros_like(dv)
-    for copy in copies:
-        copy.wait()
     first = pl.ds(0, TOK_TILE)
     second = pl.ds(TOK_TILE, TOK_TILE)
     stats = pl.ds(TOK_TILE, STAT_ROWS)
@@ -310,14 +233,10 @@
     width_tiles = count // (TT * TH)
     me = lax.axis_index("tile")
     my_head = lax.axis_index("head")
-    source_table, target_table = ring_tables(count)
-    source = jnp.asarray(source_table)[me]
-    target = jnp.asarray(target_table)[me]
-    onehot = (source[:, None] == jnp.arange(count, dtype=jnp.int32)[None, :]).astype(jnp.int32)
-    rel_tiles = jnp.sum(onehot * slot_tiles[None, :], 1)
-    allowed = near_tiles(rel_tiles, rel_tiles, width_tiles)
-
-    out_weights = head_gather_doubling(out_weight, heads)
+    allowed = near_tiles(slot_tiles, slot_tiles, width_tiles)
+    mine_allowed = lax.dynamic_slice_in_dim(allowed, me, 1, 0)
+
+    out_weights = lax.all_gather(out_weight, "head")
 
     bf16, f32 = jnp.bfloat16, jnp.float32
     normed, kv, qq = pl.pallas_call(
@@ -333,24 +252,13 @@
         name="project",
     )(tokens, mod_shift[None, :], mod_scale[None, :], qkv_weight)
 
-    kv_all = ring_gather(kv, count)
-    qq_all = ring_gather(qq, count)
+    kv_all = lax.all_gather(kv, "tile")
+    qq_all = lax.all_gather(qq, "tile")
 
     mine = lax.dynamic_slice_in_dim(normed, my_head * quarter, quarter, 0)
-    slices = []
-    for index, rel in enumerate(rel_offsets(count)):
-        piece = lax.dynamic_slice_in_dim(mine, target[index] * part, part, 1)
-        if rel:
-            piece = lax.ppermute(piece, "tile", shift_perm(count, -rel))
-        slices.append(piece)
-    slab = jnp.stack(slices, 0)
-    slabs = head_gather_doubling(slab, heads)
-    normed_part = jnp.zeros((count, heads, quarter, part), bf16)
-    for mask in range(heads):
-        normed_part = lax.dynamic_update_slice(
-            normed_part, slabs[mask][:, None], (0, my_head ^ mask, 0, 0)
-        )
-    normed_part = normed_part.reshape(count, TOK_TILE, part)
+    mine = mine.reshape(quarter, count, part).transpose(1, 0, 2)
+    slab = lax.all_to_all(mine, "tile", 0, 0, tiled=True)
+    normed_part = lax.all_gather(slab, "head", axis=1, tiled=True)
 
     attended, inverse = pl.pallas_call(
         functools.partial(attend_kernel, count),
@@ -358,7 +266,7 @@
             jax.ShapeDtypeStruct((TOK_TILE, HD), bf16),
             jax.ShapeDtypeStruct((1, TOK_TILE), f32),
         ),
-        in_specs=[pl.BlockSpec(memory_space=pltpu.SMEM)] + [vmem()] * (1 + count),
+        in_specs=[pl.BlockSpec(memory_space=pltpu.SMEM)] + [vmem()] * 2,
         out_specs=(vmem(),) * 2,
         scratch_shapes=[
             pltpu.VMEM((count, TOK_TILE, TOK_TILE), f32),
@@ -367,9 +275,9 @@
         ],
         compiler_params=params(),
         name="attend",
-    )(allowed, qq, *kv_all)
-
-    attended_all = head_gather_direct(attended, heads)
+    )(mine_allowed, qq, kv_all)
+
+    attended_all = lax.all_gather(attended, "head")
 
     chunk = 512
     row = pl.BlockSpec((1, chunk), lambda j: (0, j))
@@ -386,8 +294,11 @@
             row,
             pl.BlockSpec((TOK_TILE, chunk), lambda j: (0, j)),
         ]
-        + [whole_att] * heads
-        + [pl.BlockSpec((HD, chunk), lambda j: (0, j))] * heads,
+        + [whole_att, pl.BlockSpec((HD, chunk), lambda j: (0, j))]
+        + [
+            pl.BlockSpec((heads, TOK_TILE, HD), lambda j: (0, 0, 0)),
+            pl.BlockSpec((heads, HD, chunk), lambda j: (0, 0, j)),
+        ],
         out_specs=(
             pl.BlockSpec((TOK_TILE + STAT_ROWS, HD), lambda j: (0, 0)),
             pl.BlockSpec((HD, chunk), lambda j: (0, j)),
@@ -395,42 +306,33 @@
         scratch_shapes=[pltpu.VMEM((TOK_TILE, HD), f32)],
         compiler_params=params(),
         name="branch",
-    )(inverse, mod_gate[None, :], teacher, *attended_all, *out_weights)
-
-    ga_all = ring_gather(grad_att, count)
+    )(inverse, mod_gate[None, :], teacher, attended, out_weight, attended_all, out_weights)
+
+    ga_all = lax.all_gather(grad_att, "tile")
 
     top = jnp.max(jnp.abs(out_term), 0, keepdims=True)
     power = jnp.floor(jnp.log2(jnp.clip(top, 2.0**-100, 2.0**100))) - 10.0
     scaled = jnp.concatenate(
         [out_term * jnp.exp2(-power), jnp.broadcast_to(power, (16, features))], 0
     ).astype(jnp.float16)
-    out_grad = lax.dynamic_slice_in_dim(out_term, me * part, part, 1)
-    for index, rel in enumerate(rel_offsets(count)):
-        if rel:
-            piece = lax.dynamic_slice_in_dim(scaled, target[index] * part, part, 1)
-            piece = lax.ppermute(piece, "tile", shift_perm(count, -rel)).astype(f32)
-            out_grad += piece[:HD] * jnp.exp2(piece[HD : HD + 1])
-
-    hbm = pl.BlockSpec(memory_space=pl.ANY)
+    pieces = scaled.reshape(HD + 16, count, part).transpose(1, 0, 2)
+    pieces = lax.all_to_all(pieces, "tile", 0, 0, tiled=True).astype(f32)
+    out_grad = jnp.sum(pieces[:, :HD] * jnp.exp2(pieces[:, HD : HD + 1]), 0)
+
     qkv_grad = pl.pallas_call(
         functools.partial(backward_kernel, count),
         out_shape=jax.ShapeDtypeStruct((part, 3 * HD), f32),
-        in_specs=[pl.BlockSpec(memory_space=pltpu.SMEM)] + [hbm] * (3 * count + 1),
+        in_specs=[pl.BlockSpec(memory_space=pltpu.SMEM)] + [vmem()] * 4,
         out_specs=vmem(),
         scratch_shapes=[
-            pltpu.VMEM((count, 2 * TOK_TILE, HD), bf16),
-            pltpu.VMEM((count, 3 * TOK_TILE + STAT_ROWS, HD), bf16),
-            pltpu.VMEM((count, TOK_TILE + STAT_ROWS, HD), bf16),
-            pltpu.VMEM((count, TOK_TILE, part), bf16),
             pltpu.VMEM((HD, TOK_TILE), f32),
             pltpu.VMEM((count, TOK_TILE, HD), f32),
             pltpu.VMEM((count, TOK_TILE, HD), f32),
             pltpu.VMEM((count, TOK_TILE, 3 * HD), bf16),
-            pltpu.SemaphoreType.DMA((3 * count + 1,)),
         ],
         compiler_params=params(),
         name="backward",
-    )(allowed, *kv_all, *qq_all, *ga_all, normed_part)
+    )(allowed, kv_all, qq_all, ga_all, normed_part)
     return (qkv_grad, out_grad)
 
 

time: 208 us -> 235 us (1.13)
  blocking collectives: 0 us -> 97.2 us
  starting transfers between devices: 57.2 us -> 5.18 us
  local copies, waits for them, and re-layouts: 15.5 us -> 2.24 us
  waiting for transfers between devices: 71 us -> 58.5 us
  between operations: 6.46 us -> 13.9 us
    ppermute x44 -> x0, waiting for transfers between devices: 71 us -> none  [the longest x7 26.8 us: per_device(): piece = lax.ppermute(piece, 'tile', shift_perm(count, -rel)).astype(f32)]
    all_gather x0 -> x2, blocking collectives: none -> 67.2 us  [the longest x1 58.5 us: per_device(): ga_all = lax.all_gather(grad_att, 'tile')]
    ppermute x44 -> x0, starting transfers between devices: 57.2 us -> none  [the longest x7 20.5 us: per_device(): piece = lax.ppermute(piece, 'tile', shift_perm(count, -rel))]
    all_gather x0 -> x4, waiting for transfers between devices: none -> 57.1 us  [the longest x1 22.1 us: per_device(): normed_part = lax.all_gather(slab, 'head', axis=1, tiled=True)]
    all_to_all x0 -> x1, blocking collectives: none -> 30.1 us  [per_device(): slab = lax.all_to_all(mine, 'tile', 0, 0, tiled=True)]
    unnamed x71 -> x9, local copies, waits for them, and re-layouts: 7.3 us -> 0.33 us
    all_to_all x0 -> x1, starting transfers between devices: none -> 5.03 us  [per_device(): pieces = lax.all_to_all(pieces, 'tile', 0, 0, tiled=True).astype(f32)]
    dynamic_update_slice x4 -> x0, local copies, waits for them, and re-layouts: 3.59 us -> none  [per_device(): lax.dynamic_update_slice(normed_part, slabs[mask][:, None], (0, my_head ^...]
  transfers between devices with their start and end apart: 44 -> 5, of which waited for: 25 -> 3; matrix products, arithmetic and copies ran while one was open for 8% -> 2% of each run, Pallas kernels for 6% -> 20%
where the time goes in v2:
time: 235 us; the launch traced here: 234 us
  blocking collectives  97.2 us (41%)
  waiting for transfers between devices  58.5 us (25%)
  Pallas kernels  53.1 us (23%)
  between operations  13.9 us (6%)
  starting transfers between devices  5.18 us (2%)
  other arithmetic  3.98 us (2%)
    all_gather x1, blocking collectives, per_device(): ga_all = lax.all_gather(grad_att, 'tile')  58.5 us
    pallas_call x1, Pallas kernels, per_device(): pl.pallas_call(functools.partial(backward_kernel, count), out_shape=jax.S...  33.6 us
    all_to_all x1, blocking collectives, per_device(): slab = lax.all_to_all(mine, 'tile', 0, 0, tiled=True)  30.1 us
    all_gather x1, waiting for transfers between devices, per_device(): normed_part = lax.all_gather(slab, 'head', axis=1, tiled=True)  22.1 us
    all_gather x1, waiting for transfers between devices, per_device(): kv_all = lax.all_gather(kv, 'tile')  18.8 us
    all_gather x1, waiting for transfers between devices, per_device(): out_weights = lax.all_gather(out_weight, 'head')  16.2 us
    pallas_call x1, Pallas kernels, per_device(): pl.pallas_call(functools.partial(branch_kernel, heads), grid=(features //...  8.82 us
    all_gather x1, blocking collectives, per_device(): attended_all = lax.all_gather(attended, 'head')  8.67 us
  transfers between devices with their start and end apart: 5, of which 3 were waited for; matrix products, arithmetic and copies ran while one was open for 2% of the time, Pallas kernels for 20%

profile of v2, /device:TPU:0, one launch (start us, length us, event | category | flops | bytes accessed | tf_op | source)
XLA Modules:
  0.0 234.1 jit_solution(5425318170451653214)
XLA Ops:
  7.2 0.0 all-gather.12.cloned.1.call-start
  7.2 6.2 %project.1 = (bf16[384,3072]{1,0:T(8,128)(2,1)}, bf16[768,128]{1,0:T(8,128)(2,1)}, bf16[1184,128]{1,0:T(8,128)(2,1)}) custom-call(bf16[384,3072]{1,0:T(8,128)(2,1)} %tok_ref.1, f32[1,3072]{1,0:T(1,128)} %bitcast.35, f32[1,3072]{1,0:T(1,128)} %bitcast.36, bf16[3072,384]{1,0:T(8,128)(2,1)} %w_ref.1), custom_call_target="tpu_custom_call" | custom-call | tf_op jit(solution)/shard_map/project/pallas_call | solution.py:242
  13.4 0.0 all-gather.12.cloned.1.call-update
  13.4 0.0 all-gather.16.cloned.1.call-start
  13.5 0.7 all-gather.16.cloned.1.call-update
  14.2 0.0 all-gather.14.cloned.1.call-start
  14.2 0.7 all-gather.14.cloned.1.call-update
  14.9 0.0 all-gather.10.cloned.1.call-start
  15.0 1.1 constant_dynamic-slice_fusion
  16.1 0.0 copy-start.3
  16.1 0.1 copy.20
  16.2 30.1 %all_to_all.10 = bf16[8,96,384]{2,1,0:T(8,128)(2,1)} all-to-all(bf16[8,96,384]{2,1,0:T(8,128)(2,1)S(1)} %bitcast.32), channel_id=1, replica_groups=mesh['tile'=8,'head'=4] {'tile'}, dimensions={0} | all-to-all | bytes 1179648 | tf_op jit(solution)/shard_map/all_to_all | solution.py:260
  46.2 0.0 all-gather.10.cloned.1.call-update
  46.3 0.0 copy-done.3
  46.3 0.1 fusion.5.allowed_ref
  46.4 0.0 copy-start.2
  46.4 0.5 constant_dynamic-slice_fusion.1.allowed_ref
  46.9 18.8 %all-gather.12.cloned.1.call-done = bf16[6144,128]{1,0:T(8,128)(2,1)} async-done(((bf16[768,128]{1,0:T(8,128)(2,1)}), bf16[6144,128]{1,0:T(8,128)(2,1)}) %all-gather.12.cloned.1.call-update) | async-done | bytes 1572880 | tf_op jit(solution)/shard_map/all_gather | solution.py:255
  65.7 4.5 %attend.1 = (bf16[384,128]{1,0:T(8,128)(2,1)}, f32[1,384]{1,0:T(1,128)}) custom-call(s32[1,8]{1,0:T(1,128)} %constant_dynamic-slice_fusion.1.allowed_ref, bf16[1184,128]{1,0:T(8,128)(2,1)} %get-tuple-element.10.q_ref, bf16[8,768,128]{2,1,0:T(8,128)(2,1)} %bitcast.24), custom_call_target="tpu_custom_call" | custom-call | tf_op jit(solution)/shard_map/attend/pallas_call | solution.py:263
  70.2 8.7 %all-gather.2 = bf16[1536,128]{1,0:T(8,128)(2,1)} all-gather(bf16[384,128]{1,0:T(8,128)(2,1)} %get-tuple-element.12.refs_0_), channel_id=4, replica_groups=mesh['tile'=8,'head'=4] {'head'}, dimensions={0}, use_global_device_ids=true | all-gather | bytes 491520 | tf_op jit(solution)/shard_map/all_gather | solution.py:280
  78.8 16.2 %all-gather.16.cloned.1.call-done = bf16[512,3072]{1,0:T(8,128)(2,1)} async-done(((bf16[128,3072]{1,0:T(8,128)(2,1)}), bf16[512,3072]{1,0:T(8,128)(2,1)}) %all-gather.16.cloned.1.call-update) | async-done | bytes 3145744 | tf_op jit(solution)/shard_map/all_gather | solution.py:239
  95.0 8.8 %branch.1 = (bf16[416,128]{1,0:T(8,128)(2,1)}, f32[128,3072]{1,0:T(8,128)}) custom-call(f32[1,384]{1,0:T(1,128)} %get-tuple-element.11.inv_ref, f32[1,3072]{1,0:T(1,128)} %bitcast.37, bf16[384,3072]{1,0:T(8,128)(2,1)} %teacher_ref.1, bf16[384,128]{1,0:T(8,128)(2,1)} %get-tuple-element.12.refs_0_, bf16[128,3072]{1,0:T(8,128)(2,1)} %refs_1_.1, ...), custom_call_target="tpu_custom_call" | custom-call | tf_op jit(solution)/shard_map/branch/pallas_call | solution.py:285
  103.9 0.0 copy-done.2
  103.9 0.0 copy-start
  103.9 1.7 abs_reduce_fusion
  105.6 0.3 copy-done
  105.9 0.1 multiply_convert_fusion
  106.0 0.2 copy.19
  106.2 0.0 copy-start.1
  106.3 1.1 maximum_bitcast_fusion
  107.4 5.0 %all-to-all-start.1 = ((f16[8,144,384]{2,1,0:T(8,128)(2,1)}), f16[8,144,384]{2,1,0:T(8,128)(2,1)S(1)}, u32[]{:S(2)}, u32[]{:S(2)}) async-start(f16[8,144,384]{2,1,0:T(8,128)(2,1)} %maximum_bitcast_fusion), calls=%async_computation.1 | async-start | bytes 1769472 | tf_op jit(solution)/shard_map/all_to_all | solution.py:319
  112.4 0.0 copy-done.1
  112.4 58.5 %all-gather.4 = bf16[3328,128]{1,0:T(8,128)(2,1)} all-gather(bf16[416,128]{1,0:T(8,128)(2,1)S(1)} %copy-done.1), channel_id=6, replica_groups=mesh['tile'=8,'head'=4] {'tile'}, dimensions={0}, use_global_device_ids=true | all-gather | bytes 958464 | tf_op jit(solution)/shard_map/all_gather | solution.py:311
  170.9 0.0 all-gather.14.cloned.1.call-done
  170.9 22.1 %all-gather.10.cloned.1.call-done.nb = bf16[8,384,384]{2,1,0:T(8,128)(2,1)} async-done(((bf16[8,96,384]{2,1,0:T(8,128)(2,1)}), bf16[8,384,384]{2,1,0:T(8,128)(2,1)}) %all-gather.10.cloned.1.call-update) | async-done | bytes 2359312 | tf_op jit(solution)/shard_map/all_gather | solution.py:261
  193.0 33.6 %backward.1 = f32[384,384]{1,0:T(8,128)} custom-call(s32[8,8]{1,0:T(8,128)} %copy-done.2, bf16[8,768,128]{2,1,0:T(8,128)(2,1)} %bitcast.25, bf16[8,1184,128]{2,1,0:T(8,128)(2,1)} %bitcast.30, bf16[8,416,128]{2,1,0:T(8,128)(2,1)} %bitcast.26, bf16[8,384,384]{2,1,0:T(8,128)(2,1)} %all-gather.10.cloned.1.call-done.nb), custom_call_target="tpu_custom_call" | custom-call | tf_op jit(solution)/shard_map/backward/pallas_call | solution.py:322
  226.6 0.0 all-to-all-done.1
  226.6 0.1 convert_element_type.9
  226.8 0.8 fusion
  (6 shorter events, 0.1 us)
Async XLA Ops:
  7.2 58.5 %all-gather.12.cloned.1.call-start = ((), (), s32[]{:S(2)}) async-start(), calls=%async_computation.3 | async-start | bytes 1769472 | tf_op jit(solution)/shard_map/all_gather | solution.py:255
  13.4 81.6 %all-gather.16.cloned.1.call-start = ((), (), s32[]{:S(2)}) async-start(), calls=%async_computation.5 | async-start | bytes 3932160 | tf_op jit(solution)/shard_map/all_gather | solution.py:239
  14.2 156.7 %all-gather.14.cloned.1.call-start = ((), (), s32[]{:S(2)}) async-start(), calls=%async_computation.4 | async-start | bytes 2727936 | tf_op jit(solution)/shard_map/all_gather | solution.py:256
  14.9 178.1 %all-gather.10.cloned.1.call-start = ((), (), s32[]{:S(2)}) async-start(), calls=%async_computation.2 | async-start | bytes 2949120 | tf_op jit(solution)/shard_map/all_gather | solution.py:261
  16.1 30.2 %copy-start.3 = (s32[8]{0:T(128)S(1)}, s32[8]{0:T(128)}, u32[]{:S(2)}) copy-start(s32[8]{0:T(128)} %param.15) | copy-start | bytes 100
  46.4 57.5 %copy-start.2 = (s32[8,8]{1,0:T(8,128)}, s32[8,8]{1,0:T(8,128)S(1)}, u32[]{:S(2)}) copy-start(s32[8,8]{1,0:T(8,128)S(1)} %fusion.5.allowed_ref) | copy-start | bytes 772
  103.9 2.0 copy-start
  106.2 6.2 %copy-start.1 = (bf16[416,128]{1,0:T(8,128)(2,1)S(1)}, bf16[416,128]{1,0:T(8,128)(2,1)}, u32[]{:S(2)}) copy-start(bf16[416,128]{1,0:T(8,128)(2,1)} %get-tuple-element.13) | copy-start | bytes 319492
  107.4 119.2 %all-to-all-start.1 = ((f16[8,144,384]{2,1,0:T(8,128)(2,1)}), f16[8,144,384]{2,1,0:T(8,128)(2,1)S(1)}, u32[]{:S(2)}, u32[]{:S(2)}) async-start(f16[8,144,384]{2,1,0:T(8,128)(2,1)} %maximum_bitcast_fusion), calls=%async_computation.1 | async-start | bytes 1769472 | tf_op jit(solution)/shard_map/all_to_all | solution.py:319
Sparse Core Ops, SparseCore 0:
  13.5 52.0 all-gather.11
  67.2 27.7 all-gather.15
  97.8 71.5 all-gather.13
  170.8 22.1 all-gather.9

commit v3 on v1

v3 whole, which is shorter than its diff:
```python
import functools
import math

import jax
import jax.numpy as jnp
import numpy as np
from jax import lax
from jax.experimental import pallas as pl
from jax.experimental.pallas import tpu as pltpu
from jax.sharding import PartitionSpec as P

HD = 128
TOK_TILE = 384
LANE_ROWS = TOK_TILE // HD
TT = 1
TH = 4


EPS_NORM = 1e-05
EPS_ROOT = 1e-06
LOSS_WEIGHT = 32.0
EXP_SCALE = math.log2(math.e) / math.sqrt(HD)
ATT_SCALE = 1.0 / math.sqrt(HD)
STAT_ROWS = 32
VMEM_BYTES = 56 * 1024 * 1024

NN = (((1,), (0,)), ((), ()))
NT = (((1,), (1,)), ((), ()))
TN = (((0,), (0,)), ((), ()))


def mm(a, b, dims):
    return lax.dot_general(a, b, dims, preferred_element_type=jnp.float32)


def ring_order(count):
    return [*range(0, count, 2), *range(count - 1 - (count % 2), 0, -2)]


def rel_offsets(count):
    offsets = [0]
    for step in range(1, count // 2 + 1):
        offsets.append(-step)
        if len(offsets) < count:
            offsets.append(step)
    return offsets[:count]


def ring_table(count):
    order = ring_order(count)
    pos = [order.index(slot) for slot in range(count)]
    rels = rel_offsets(count)
    return np.array([[order[(pos[s] + rel) % count] for rel in rels] for s in range(count)], np.int32)


def shift_perm(count, offset):
    order = ring_order(count)
    return [(order[p], order[(p + offset) % count]) for p in range(count)]


def ring_gather(block, count):
    up, down = [block], [block]
    for _ in range(count // 2):
        up.append(lax.ppermute(up[-1], "tile", shift_perm(count, 1)))
    for _ in range((count - 1) // 2):
        down.append(lax.ppermute(down[-1], "tile", shift_perm(count, -1)))
    out = []
    for rel in rel_offsets(count):
        out.append(up[-rel] if rel <= 0 else down[rel])
    return out


def xor_perm(count, mask):
    return [(h, h ^ mask) for h in range(count)]


def head_gather_direct(block, count):
    return [block] + [lax.ppermute(block, "head", xor_perm(count, m)) for m in range(1, count)]


def near_tiles(first_tiles, second_tiles, width_tiles):

    def coords(ids):
        return (ids // (TH * width_tiles), ids // width_tiles % TH, ids % width_tiles)

    ta, ha, wa = coords(first_tiles[:, None])
    tb, hb, wb = coords(second_tiles[None, :])
    close = (jnp.abs(ta - tb) <= 1) & (jnp.abs(ha - hb) <= 1) & (jnp.abs(wa - wb) <= 1)
    return close.astype(jnp.int32)


def near_lists(close):
    count = close.shape[0]
    before = jnp.sum(
        close[:, None, :] * (jnp.arange(count)[None, :] < jnp.arange(count)[:, None])[None], 2
    )
    at = (before[:, None, :] == jnp.arange(count)[None, :, None]) & (close[:, None, :] != 0)
    lists = jnp.sum(at * jnp.arange(count, dtype=jnp.int32)[None, None, :], 2)
    return jnp.concatenate([lists, jnp.sum(close, 1, keepdims=True)], 1).astype(jnp.int32)


def split3(row):
    hi = row.astype(jnp.bfloat16).astype(jnp.float32)
    rest = row - hi
    mid = rest.astype(jnp.bfloat16).astype(jnp.float32)
    return [hi, mid, rest - mid]


def pack_rows(rows):
    pieces = [part for row in rows for part in split3(row)]
    pieces.append(jnp.zeros((STAT_ROWS - len(pieces), HD), jnp.float32))
    return jnp.concatenate(pieces, 0).astype(jnp.bfloat16)


def unpack_rows(packed, index):
    wide = packed.astype(jnp.float32)
    rows = []
    for chunk in range(LANE_ROWS):
        at = (index * LANE_ROWS + chunk) * 3
        rows.append(wide[at : at + 1] + wide[at + 1 : at + 2] + wide[at + 2 : at + 3])
    return jnp.concatenate(rows, 1)


def lane_chunks(row):
    return [row[:, c * HD : (c + 1) * HD] for c in range(LANE_ROWS)]


def project_kernel(tok_ref, shift_ref, scale_ref, w_ref, normed_ref, kv_ref, q_ref, lo_ref):
    query_rows, key_rows = [], []
    for chunk in range(LANE_ROWS):
        rows = pl.ds(chunk * HD, HD)
        values_in = tok_ref[rows, :].astype(jnp.float32)
        center = values_in - jnp.mean(values_in, -1, keepdims=True)
        spread = jnp.mean(center * center, -1, keepdims=True)
        normed = (
            center * lax.rsqrt(spread + EPS_NORM) * (1.0 + scale_ref[...]) + shift_ref[...]
        ).astype(jnp.bfloat16)
        normed_ref[rows, :] = normed
        projected = mm(normed, w_ref[...], NN)
        query, key, value = (projected[:, c * HD : (c + 1) * HD] for c in range(3))
        rq = lax.rsqrt(jnp.mean(query * query, -1, keepdims=True) + EPS_ROOT)
        rk = lax.rsqrt(jnp.mean(key * key, -1, keepdims=True) + EPS_ROOT)
        query, key = query * rq, key * rk
        query_b, key_b = query.astype(jnp.bfloat16), key.astype(jnp.bfloat16)
        q_ref[rows, :] = query_b
        lo_ref[rows, :] = (
            query - query_b.astype(jnp.float32)
        ).astype(jnp.bfloat16)
        lo_ref[pl.ds(TOK_TILE + chunk * HD, HD), :] = (
            key - key_b.astype(jnp.float32)
        ).astype(jnp.bfloat16)
        kv_ref[rows, :] = key_b
        kv_ref[pl.ds(TOK_TILE + chunk * HD, HD), :] = value.astype(jnp.bfloat16)
        query_rows.append(jnp.broadcast_to(rq, (HD, HD)).T[0:1])
        key_rows.append(jnp.broadcast_to(rk, (HD, HD)).T[0:1])
    lo_ref[pl.ds(2 * TOK_TILE, STAT_ROWS), :] = pack_rows(query_rows + key_rows)


def attend_kernel(count, allowed_ref, q_ref, *refs):
    kv_refs = refs[:count]
    att_ref, inv_ref, expo, totals, acc = refs[count:]
    query = q_ref[...]
    totals[...] = jnp.zeros_like(totals)
    acc[...] = jnp.zeros_like(acc)
    for r in range(count):

        @pl.when(allowed_ref[0, r] != 0)
        def _():
            scores = mm(kv_refs[r][pl.ds(0, TOK_TILE), :], query, NT)
            part = jnp.exp2(scores * EXP_SCALE)
            expo[r] = part
            totals[...] += jnp.sum(part, 0, keepdims=True)

    inverse = 1.0 / totals[...]
    inv_ref[...] = inverse
    for r in range(count):

        @pl.when(allowed_ref[0, r] != 0)
        def _():
            probs = (expo[r] * inverse).astype(jnp.bfloat16)
            acc[...] += mm(kv_refs[r][pl.ds(TOK_TILE, TOK_TILE), :], probs, TN)

    att_ref[...] = acc[...].T.astype(jnp.bfloat16)


def branch_kernel(heads, q_ref, inv_ref, gate_ref, teacher_ref, *refs):
    att_refs = refs[:heads]
    my_w, all_w, my_head, qd_ref, out_ref, acc = refs[heads:]
    step = pl.program_id(0)

    @pl.when(step == 0)
    def _():
        acc[...] = jnp.zeros_like(acc)

    branch = mm(att_refs[0][...], my_w[...], NN)
    for mask in range(1, heads):
        branch += mm(att_refs[mask][...], all_w[my_head[0] ^ mask], NN)
    gate = gate_ref[...]
    residual = LOSS_WEIGHT * (gate * branch - teacher_ref[...].astype(jnp.float32))
    grad = (gate * residual).astype(jnp.bfloat16)
    out_ref[...] = mm(att_refs[0][...], grad, TN)
    acc[...] += mm(grad, my_w[...], NT)

    @pl.when(step == pl.num_programs(0) - 1)
    def _():
        grad_att = acc[...].astype(jnp.bfloat16)
        qd_ref[pl.ds(0, TOK_TILE), :] = q_ref[...]
        qd_ref[pl.ds(TOK_TILE, TOK_TILE), :] = grad_att
        product = grad_att.astype(jnp.float32) * att_refs[0][...].astype(jnp.float32)
        delta = jnp.sum(product.T, 0, keepdims=True)
        qd_ref[pl.ds(2 * TOK_TILE, STAT_ROWS), :] = pack_rows(
            lane_chunks(inv_ref[...]) + lane_chunks(delta)
        )


FIRST = pl.ds(0, TOK_TILE)
SECOND = pl.ds(TOK_TILE, TOK_TILE)
STATS = pl.ds(2 * TOK_TILE, STAT_ROWS)


def query_tile(row, near_ref, kv, qd_ref, dq, dk, dv):
    query = qd_ref[FIRST, :]
    grad = qd_ref[SECOND, :]
    packed = qd_ref[STATS, :]
    inverse, delta = unpack_rows(packed, 0), unpack_rows(packed, 1)
    count = near_ref.shape[1] - 1
    near = near_ref[row, count]

    def terms(keys):
        scores = [mm(kv[j, FIRST, :], query, NT) for j in keys]
        grad_probs = [mm(kv[j, SECOND, :], grad, NT) for j in keys]
        probs = [jnp.exp2(s * EXP_SCALE) * inverse for s in scores]
        grad_scores = [
            (p * (g - delta)).astype(jnp.bfloat16) for p, g in zip(probs, grad_probs)
        ]
        value_terms = [mm(p.astype(jnp.bfloat16), grad, NN) for p in probs]
        key_terms = [mm(g, query, NN) for g in grad_scores]
        query_terms = [mm(kv[j, FIRST, :], g, TN) for j, g in zip(keys, grad_scores)]
        total = query_terms[0]
        for term in query_terms[1:]:
            total += term
        dq[...] += total
        for j, value_term, key_term in zip(keys, value_terms, key_terms):
            dv[j] += value_term
            dk[j] += key_term

    dq[...] = jnp.zeros(dq.shape, jnp.float32)

    def two(at, carry):
        terms([near_ref[row, 2 * at], near_ref[row, 2 * at + 1]])
        return carry

    lax.fori_loop(0, near // 2, two, 0)

    @pl.when(near % 2 == 1)
    def _():
        terms([near_ref[row, near - 1]])


def start_all(copies):
    for copy in copies:
        copy.start()
    return copies


def wait_all(copies):
    for copy in copies:
        copy.wait()


def chunk_kernel(count, members, chained, near_ref, *refs):
    size = len(members)
    kv_in, qd_in = refs[:count], refs[count : count + size]
    refs = refs[count + size :]
    if chained:
        prev_k, prev_v, dq_ref, dk_ref, dv_ref, kv, sems, before_k, before_v = refs
    else:
        dq_ref, dk_ref, dv_ref, kv, sems = refs
    loads = start_all(
        [pltpu.make_async_copy(kv_in[r], kv.at[r], sems.at[r]) for r in range(count)]
    )
    if chained:
        late = start_all(
            [
                pltpu.make_async_copy(prev_k, before_k, sems.at[count]),
                pltpu.make_async_copy(prev_v, before_v, sems.at[count + 1]),
            ]
        )
    dk_ref[...] = jnp.zeros(dk_ref.shape, jnp.float32)
    dv_ref[...] = jnp.zeros(dv_ref.shape, jnp.float32)
    wait_all(loads)
    for at, row in enumerate(members):
        query_tile(row, near_ref, kv, qd_in[at], dq_ref.at[at], dk_ref, dv_ref)
    if chained:
        wait_all(late)
        dk_ref[...] += before_k[...]
        dv_ref[...] += before_v[...]


def final_kernel(count, members, near_ref, source_ref, *refs):
    size = len(members)
    kv_in, qd_in, refs = refs[:count], refs[count : 2 * count], refs[2 * count :]
    dq_in, refs = refs[: count - size], refs[count - size :]
    prev_k, prev_v, lo_in, nb_in, out_ref, kv, qd, dq, dk, dv, lo, nb, grads, sems = refs
    at = iter(range(4 * count + 4))

    def copy(src, dst):
        return pltpu.make_async_copy(src, dst, sems.at[next(at)])

    loads = start_all(
        [copy(kv_in[r], kv.at[r]) for r in range(count)]
        + [copy(qd_in[r], qd.at[r]) for r in members]
        + [copy(prev_k, dk), copy(prev_v, dv)]
    )
    rest = [r for r in range(count) if r not in members]
    late = start_all(
        [copy(qd_in[r], qd.at[r]) for r in rest]
        + [copy(dq_in[r], dq.at[pl.ds(r, 1)]) for r in rest]
        + [copy(lo_in, lo), copy(nb_in, nb)]
    )
    wait_all(loads)
    for row in members:
        query_tile(row, near_ref, kv, qd.at[row], dq.at[row], dk, dv)
    wait_all(late)

    def finish(r, carry):
        slot = source_ref[r]
        query_unit = qd[r, FIRST, :].astype(jnp.float32) + lo[slot, FIRST, :].astype(jnp.float32)
        key_unit = kv[r, FIRST, :].astype(jnp.float32) + lo[slot, SECOND, :].astype(jnp.float32)
        packed = lo[slot, STATS, :]
        grads[r, :, pl.ds(0, HD)] = root_back(
            dq[r].T * ATT_SCALE, query_unit, unpack_rows(packed, 0)
        )
        grads[r, :, pl.ds(HD, HD)] = root_back(dk[r] * ATT_SCALE, key_unit, unpack_rows(packed, 1))
        grads[r, :, pl.ds(2 * HD, HD)] = dv[r].astype(jnp.bfloat16)
        return carry

    lax.fori_loop(0, count, finish, 0)
    out_ref[...] = jnp.zeros_like(out_ref)

    def weight(r, carry):
        out_ref[...] += mm(nb[source_ref[r]], grads[r], TN)
        return carry

    lax.fori_loop(0, count, weight, 0)


def root_back(grad_unit, unit_value, factor_row):
    factor = jnp.broadcast_to(factor_row, (HD, TOK_TILE)).T
    inner = jnp.mean(grad_unit * unit_value, -1, keepdims=True)
    return (factor * (grad_unit - unit_value * inner)).astype(jnp.bfloat16)


def vmem():
    return pl.BlockSpec(memory_space=pltpu.VMEM)


def params():
    return pltpu.CompilerParams(vmem_limit_bytes=VMEM_BYTES)


def per_device(
    count, heads, tokens, mod_shift, mod_scale, mod_gate, qkv_weight, out_weight, teacher, slot_tiles
):
    features = tokens.shape[1]
    part = features // count
    quarter = TOK_TILE // heads
    width_tiles = count // (TT * TH)
    me = lax.axis_index("tile")
    my_head = lax.axis_index("head")
    source_table = ring_table(count)
    source = jnp.asarray(source_table)[me]
    onehot = (source[:, None] == jnp.arange(count, dtype=jnp.int32)[None, :]).astype(jnp.int32)
    rel_tiles = jnp.sum(onehot * slot_tiles[None, :], 1)
    allowed = near_tiles(rel_tiles, rel_tiles, width_tiles)

    near = near_lists(allowed)

    out_weights = lax.all_gather(out_weight, "head")
    my_weight = out_weight

    bf16, f32 = jnp.bfloat16, jnp.float32
    normed, kv, query, low = pl.pallas_call(
        project_kernel,
        out_shape=(
            jax.ShapeDtypeStruct((TOK_TILE, features), bf16),
            jax.ShapeDtypeStruct((2 * TOK_TILE, HD), bf16),
            jax.ShapeDtypeStruct((TOK_TILE, HD), bf16),
            jax.ShapeDtypeStruct((2 * TOK_TILE + STAT_ROWS, HD), bf16),
        ),
        in_specs=[vmem()] * 4,
        out_specs=(vmem(),) * 4,
        compiler_params=params(),
        name="project",
    )(tokens, mod_shift[None, :], mod_scale[None, :], qkv_weight)

    kv_all = ring_gather(kv, count)
    low, normed, *kv_all = lax.optimization_barrier((low, normed, *kv_all))

    attended, inverse = pl.pallas_call(
        functools.partial(attend_kernel, count),
        out_shape=(
            jax.ShapeDtypeStruct((TOK_TILE, HD), bf16),
            jax.ShapeDtypeStruct((1, TOK_TILE), f32),
        ),
        in_specs=[pl.BlockSpec(memory_space=pltpu.SMEM)] + [vmem()] * (1 + count),
        out_specs=(vmem(),) * 2,
        scratch_shapes=[
            pltpu.VMEM((count, TOK_TILE, TOK_TILE), f32),
            pltpu.VMEM((1, TOK_TILE), f32),
            pltpu.VMEM((HD, TOK_TILE), f32),
        ],
        compiler_params=params(),
        name="attend",
    )(allowed, query, *kv_all)

    normed, attended = lax.optimization_barrier((normed, attended))
    mine = lax.dynamic_slice_in_dim(normed, my_head * quarter, quarter, 0)
    mine = mine.reshape(quarter, count, part).transpose(1, 0, 2)
    slab = lax.all_to_all(mine, "tile", 0, 0, tiled=True)
    normed_part = lax.all_gather(slab, "head", axis=1, tiled=True)
    low_all = lax.all_gather(low, "tile")

    attended_all = head_gather_direct(attended, heads)

    chunk = 512
    row = pl.BlockSpec((1, chunk), lambda j: (0, j))
    whole_att = pl.BlockSpec((TOK_TILE, HD), lambda j: (0, 0))
    qd, out_term = pl.pallas_call(
        functools.partial(branch_kernel, heads),
        grid=(features // chunk,),
        out_shape=(
            jax.ShapeDtypeStruct((2 * TOK_TILE + STAT_ROWS, HD), bf16),
            jax.ShapeDtypeStruct((HD, features), f32),
        ),
        in_specs=[
            whole_att,
            pl.BlockSpec((1, TOK_TILE), lambda j: (0, 0)),
            row,
            pl.BlockSpec((TOK_TILE, chunk), lambda j: (0, j)),
        ]
        + [whole_att] * heads
        + [
            pl.BlockSpec((HD, chunk), lambda j: (0, j)),
            pl.BlockSpec((heads, HD, chunk), lambda j: (0, 0, j)),
            pl.BlockSpec(memory_space=pltpu.SMEM),
        ],
        out_specs=(
            pl.BlockSpec((2 * TOK_TILE + STAT_ROWS, HD), lambda j: (0, 0)),
            pl.BlockSpec((HD, chunk), lambda j: (0, j)),
        ),
        scratch_shapes=[pltpu.VMEM((TOK_TILE, HD), f32)],
        compiler_params=params(),
        name="branch",
    )(
        query,
        inverse,
        mod_gate[None, :],
        teacher,
        *attended_all,
        my_weight,
        out_weights,
        my_head.astype(jnp.int32)[None],
    )

    top = jnp.max(jnp.abs(out_term), 0, keepdims=True)
    power = jnp.floor(jnp.log2(jnp.clip(top, 2.0**-100, 2.0**100))) - 10.0
    scaled = jnp.concatenate(
        [out_term * jnp.exp2(-power), jnp.broadcast_to(power, (16, features))], 0
    ).astype(jnp.float16)
    pieces = scaled.reshape(HD + 16, count, part).transpose(1, 0, 2)
    pieces = lax.all_to_all(pieces, "tile", 0, 0, tiled=True).astype(f32)
    out_grad = jnp.sum(pieces[:, :HD] * jnp.exp2(pieces[:, HD : HD + 1]), 0)

    smem = pl.BlockSpec(memory_space=pltpu.SMEM)
    hbm = pl.BlockSpec(memory_space=pl.ANY)
    sums = jax.ShapeDtypeStruct((count, TOK_TILE, HD), f32)
    sums_vmem = pltpu.VMEM((count, TOK_TILE, HD), f32)
    kv_vmem = pltpu.VMEM((count, 2 * TOK_TILE, HD), bf16)
    qd_all, dq_all, prev = [qd], [], ()
    up, down, step = qd, qd, 0
    while True:
        step += 1
        arrived = list(range(max(0, 2 * step - 3), 2 * step - 1))
        up = lax.ppermute(up, "tile", shift_perm(count, 1))
        if 2 * step < count:
            down = lax.ppermute(down, "tile", shift_perm(count, -1))
        if 2 * step == count:
            break
        dq, *prev = pl.pallas_call(
            functools.partial(chunk_kernel, count, arrived, bool(prev)),
            out_shape=(
                jax.ShapeDtypeStruct((len(arrived), HD, TOK_TILE), f32),
                sums,
                sums,
            ),
            in_specs=[smem] + [hbm] * count + [vmem()] * len(arrived) + [hbm] * len(prev),
            out_specs=(vmem(),) * 3,
            scratch_shapes=[kv_vmem, pltpu.SemaphoreType.DMA((count + 2,))]
            + [sums_vmem] * len(prev),
            compiler_params=params(),
            name=f"backward{step}",
        )(near, *kv_all, *[qd_all[r] for r in arrived], *prev)
        dq_all += [lax.slice_in_dim(dq, k, k + 1) for k in range(len(arrived))]
        qd_all += [up, down]
    qd_all.append(up)
    members = list(range(len(dq_all), count))

    qkv_grad = pl.pallas_call(
        functools.partial(final_kernel, count, members),
        out_shape=jax.ShapeDtypeStruct((part, 3 * HD), f32),
        in_specs=[smem] * 2 + [hbm] * (2 * count + len(dq_all) + 4),
        out_specs=vmem(),
        scratch_shapes=[
            kv_vmem,
            pltpu.VMEM((count, 2 * TOK_TILE + STAT_ROWS, HD), bf16),
            pltpu.VMEM((count, HD, TOK_TILE), f32),
            sums_vmem,
            sums_vmem,
            pltpu.VMEM((count, 2 * TOK_TILE + STAT_ROWS, HD), bf16),
            pltpu.VMEM((count, TOK_TILE, part), bf16),
            pltpu.VMEM((count, TOK_TILE, 3 * HD), bf16),
            pltpu.SemaphoreType.DMA((4 * count + 4,)),
        ],
        compiler_params=params(),
        name="final",
    )(near, source, *kv_all, *qd_all, *dq_all, *prev, low_all, normed_part)
    return (qkv_grad, out_grad)


def solution(mesh):
    return jax.shard_map(
        functools.partial(per_device, mesh.shape["tile"], mesh.shape["head"]),
        mesh=mesh,
        in_specs=(
            P("tile", None),
            P(),
            P(),
            P(),
            P(None, "head"),
            P("head", None),
            P("tile", None),
            P(),
        ),
        out_specs=(P("tile", "head"), P("head", "tile")),
        check_vma=False,
    )
```

time: 208 us -> 189 us (0.909)
  starting transfers between devices: 57.2 us -> 27.2 us
  waiting for transfers between devices: 71 us -> 43.5 us
  blocking collectives: 0 us -> 24.7 us
  Pallas kernels: 53.7 us -> 63.5 us
  between operations: 6.46 us -> 14.1 us
  local copies, waits for them, and re-layouts: 15.5 us -> 8.69 us
    ppermute x20 -> x7, waiting for transfers between devices: 48.3 us -> 20.9 us  [the longest x4 20.9 us: per_device(): up = lax.ppermute(up, 'tile', shift_perm(count, 1))]
    all_to_all x0 -> x1, blocking collectives: none -> 24.7 us  [per_device(): slab = lax.all_to_all(mine, 'tile', 0, 0, tiled=True)]
    ppermute x20 -> x7, starting transfers between devices: 31.2 us -> 13 us  [the longest x4 12.8 us: per_device(): up = lax.ppermute(up, 'tile', shift_perm(count, 1))]
    ppermute x9 -> x3, starting transfers between devices: 15.3 us -> 0.76 us  [ring_gather(): down.append(lax.ppermute(down[-1], 'tile', shift_perm(count, -1)))]
    pallas_call x1 -> x4, Pallas kernels: 34.2 us -> 42.8 us  [the longest x3 25.7 us: per_device(): pl.pallas_call(functools.partial(chunk_kernel, count, arrived, bool(prev)...]
    unnamed x71 -> x47, local copies, waits for them, and re-layouts: 7.3 us -> 2.88 us
    ppermute x9 -> x3, waiting for transfers between devices: 4.19 us -> 0.01 us  [ring_gather(): down.append(lax.ppermute(down[-1], 'tile', shift_perm(count, -1)))]
    dynamic_update_slice x4 -> x0, local copies, waits for them, and re-layouts: 3.59 us -> none  [per_device(): lax.dynamic_update_slice(normed_part, slabs[mask][:, None], (0, my_head ^...]
  transfers between devices with their start and end apart: 44 -> 21, of which waited for: 25 -> 8; matrix products, arithmetic and copies ran while one was open for 8% -> 6% of each run, Pallas kernels for 6% -> 34%
where the time goes in v3:
time: 189 us; the launch traced here: 188 us
  Pallas kernels  63.5 us (34%)
  waiting for transfers between devices  43.5 us (23%)
  starting transfers between devices  27.2 us (14%)
  blocking collectives  24.7 us (13%)
  between operations  14.1 us (7%)
  local copies, waits for them, and re-layouts  8.69 us (5%)
  other arithmetic  5.99 us (3%)
    pallas_call x3, Pallas kernels, per_device(): pl.pallas_call(functools.partial(chunk_kernel, count, arrived, bool(prev)...  25.7 us
    all_to_all x1, blocking collectives, per_device(): slab = lax.all_to_all(mine, 'tile', 0, 0, tiled=True)  24.7 us
    ppermute x4, waiting for transfers between devices, per_device(): up = lax.ppermute(up, 'tile', shift_perm(count, 1))  20.9 us
    pallas_call x1, Pallas kernels, per_device(): pl.pallas_call(functools.partial(final_kernel, count, members), out_shape...  17.1 us
    ppermute x4, waiting for transfers between devices, ring_gather(): up.append(lax.ppermute(up[-1], 'tile', shift_perm(count, 1)))  16.9 us
    ppermute x4, starting transfers between devices, per_device(): up = lax.ppermute(up, 'tile', shift_perm(count, 1))  12.8 us
    pallas_call x1, Pallas kernels, per_device(): pl.pallas_call(functools.partial(branch_kernel, heads), grid=(features //...  8.92 us
    ppermute x4, starting transfers between devices, ring_gather(): up.append(lax.ppermute(up[-1], 'tile', shift_perm(count, 1)))  7.81 us
  transfers between devices with their start and end apart: 21, of which 8 were waited for; matrix products, arithmetic and copies ran while one was open for 6% of the time, Pallas kernels for 34%

profile of v3, /device:TPU:0, one launch (start us, length us, event | category | flops | bytes accessed | tf_op | source)
XLA Modules:
  0.0 187.7 jit_solution(148462557583451239)
XLA Ops:
  7.2 0.0 all-gather.8.cloned.1.call-start
  7.2 0.7 all-gather.8.cloned.1.call-update
  7.9 0.0 all-gather.10.cloned.1.call-start
  8.0 6.2 %project.1 = (bf16[384,3072]{1,0:T(8,128)(2,1)}, bf16[768,128]{1,0:T(8,128)(2,1)}, bf16[384,128]{1,0:T(8,128)(2,1)}, bf16[800,128]{1,0:T(8,128)(2,1)}) custom-call(bf16[384,3072]{1,0:T(8,128)(2,1)} %tok_ref.1, f32[1,3072]{1,0:T(1,128)} %bitcast.32, f32[1,3072]{1,0:T(1,128)} %bitcast.33, bf16[3072,384]{1,0:T(8,128)(2,1)} %w_ref.1), custom_call_target="tpu_custom_call" | custom-call | tf_op jit(solution)/shard_map/project/pallas_call | solution.py:383
  14.2 3.0 %collective-permute-start = (bf16[768,128]{1,0:T(8,128)(2,1)}, bf16[768,128]{1,0:T(8,128)(2,1)S(1)}, u32[]{:S(2)}, u32[]{:S(2)}) collective-permute-start(bf16[768,128]{1,0:T(8,128)(2,1)} %get-tuple-element.34.refs_0_), channel_id=1, source_target_pairs={{0,8},{8,16},{16,24},{24,28},{28,20},{20,12},{12,4},{4,0},{1,9},{9... | collective-permute-start | bytes 589832 | tf_op jit(solution)/shard_map/ppermute | solution.py:64
  17.2 5.0 %collective-permute-done.refs_1_ = bf16[768,128]{1,0:T(8,128)(2,1)S(1)} collective-permute-done((bf16[768,128]{1,0:T(8,128)(2,1)}, bf16[768,128]{1,0:T(8,128)(2,1)S(1)}, u32[]{:S(2)}, u32[]{:S(2)}) %collective-permute-start) | collective-permute-done | bytes 196640 | tf_op jit(solution)/shard_map/ppermute | solution.py:64
  22.2 1.8 collective-permute-start.2
  24.0 0.0 collective-permute-done.1.refs_2_
  24.0 0.2 collective-permute-start.3
  24.3 4.0 %collective-permute-done.2.refs_3_ = bf16[768,128]{1,0:T(8,128)(2,1)S(1)} collective-permute-done((bf16[768,128]{1,0:T(8,128)(2,1)S(1)}, bf16[768,128]{1,0:T(8,128)(2,1)S(1)}, u32[]{:S(2)}, u32[]{:S(2)}) %collective-permute-start.2) | collective-permute-done | bytes 196640 | tf_op jit(solution)/shard_map/ppermute | solution.py:64
  28.3 1.5 collective-permute-start.4
  29.8 0.5 collective-permute-start.5
  30.3 3.6 %collective-permute-done.4.refs_5_ = bf16[768,128]{1,0:T(8,128)(2,1)S(1)} collective-permute-done((bf16[768,128]{1,0:T(8,128)(2,1)S(1)}, bf16[768,128]{1,0:T(8,128)(2,1)S(1)}, u32[]{:S(2)}, u32[]{:S(2)}) %collective-permute-start.4) | collective-permute-done | bytes 196640 | tf_op jit(solution)/shard_map/ppermute | solution.py:64
  34.0 1.5 collective-permute-start.6
  35.5 4.2 %collective-permute-done.6.refs_7_ = bf16[768,128]{1,0:T(8,128)(2,1)S(1)} collective-permute-done((bf16[768,128]{1,0:T(8,128)(2,1)S(1)}, bf16[768,128]{1,0:T(8,128)(2,1)S(1)}, u32[]{:S(2)}, u32[]{:S(2)}) %collective-permute-start.6) | collective-permute-done | bytes 196640 | tf_op jit(solution)/shard_map/ppermute | solution.py:64
  39.7 0.0 all-gather.10.cloned.1.call-update
  39.7 0.0 all-gather.6.cloned.1.call-start
  39.7 0.7 dynamic-slice_bitcast_fusion.source_ref
  40.5 0.2 select_reduce_fusion.1
  40.7 0.7 broadcast_compare_fusion
  41.4 5.5 %attend.1 = (bf16[384,128]{1,0:T(8,128)(2,1)}, f32[1,384]{1,0:T(1,128)}) custom-call(s32[8,8]{1,0:T(8,128)} %get-tuple-element.67.allowed_ref, bf16[384,128]{1,0:T(8,128)(2,1)} %get-tuple-element.42.q_ref, bf16[768,128]{1,0:T(8,128)(2,1)} %get-tuple-element.34.refs_0_, bf16[768,128]{1,0:T(8,128)(2,1)} %copy-done.1, bf16[768,128]{1,0:T(8,128)(2,1)} %copy-done.2, ...), custom_call_target="tpu_custom_call" | custom-call | tf_op jit(solution)/shard_map/attend/pallas_call | solution.py:400
  46.9 1.1 constant_dynamic-slice_fusion
  48.0 0.1 copy.27
  48.1 24.7 %all_to_all.10 = bf16[8,96,384]{2,1,0:T(8,128)(2,1)} all-to-all(bf16[8,96,384]{2,1,0:T(8,128)(2,1)S(1)} %bitcast.29), channel_id=1, replica_groups=mesh['tile'=8,'head'=4] {'tile'}, dimensions={0} | all-to-all | bytes 1179648 | tf_op jit(solution)/shard_map/all_to_all | solution.py:420
  72.8 0.0 all-gather.6.cloned.1.call-update
  72.8 0.1 collective-permute-start.7
  72.9 1.6 collective-permute-start.8
  74.5 0.3 collective-permute-start.9
  74.7 3.8 %collective-permute-done.8.refs_2_ = bf16[384,128]{1,0:T(8,128)(2,1)S(1)} collective-permute-done((bf16[384,128]{1,0:T(8,128)(2,1)S(1)}, bf16[384,128]{1,0:T(8,128)(2,1)S(1)}, u32[]{:S(2)}, u32[]{:S(2)}) %collective-permute-start.8) | collective-permute-done | bytes 98336 | tf_op jit(solution)/shard_map/ppermute | solution.py:78
  78.5 1.2 collective-permute-done.9.refs_3_
  79.8 0.6 copy-done.19
  80.4 8.9 %branch.1 = (bf16[800,128]{1,0:T(8,128)(2,1)}, f32[128,3072]{1,0:T(8,128)}) custom-call(bf16[384,128]{1,0:T(8,128)(2,1)} %get-tuple-element.42.q_ref, f32[1,384]{1,0:T(1,128)} %get-tuple-element.43.inv_ref, f32[1,3072]{1,0:T(1,128)} %bitcast.34, bf16[384,3072]{1,0:T(8,128)(2,1)} %teacher_ref.1, bf16[384,128]{1,0:T(8,128)(2,1)} %get-tuple-element.46.refs_0_, ...), custom_call_target="tpu_custom_call" | custom-call | tf_op jit(solution)/shard_map/branch/pallas_call | solution.py:429
  89.3 1.6 abs_reduce_fusion
  90.9 0.2 copy-done
  91.2 0.1 multiply_convert_fusion
  91.3 0.2 copy.26
  91.6 1.1 maximum_bitcast_fusion
  92.7 3.5 %all-to-all-start.1 = ((f16[8,144,384]{2,1,0:T(8,128)(2,1)}), f16[8,144,384]{2,1,0:T(8,128)(2,1)S(1)}, u32[]{:S(2)}, u32[]{:S(2)}) async-start(f16[8,144,384]{2,1,0:T(8,128)(2,1)} %maximum_bitcast_fusion), calls=%async_computation.1 | async-start | bytes 1769472 | tf_op jit(solution)/shard_map/all_to_all | solution.py:472
  96.3 0.2 fusion.8
  96.4 0.1 copy.17
  96.5 1.9 %collective-permute-start.10 = (bf16[800,128]{1,0:T(8,128)(2,1)S(1)}, bf16[800,128]{1,0:T(8,128)(2,1)S(1)}, u32[]{:S(2)}, u32[]{:S(2)}) collective-permute-start(bf16[800,128]{1,0:T(8,128)(2,1)S(1)} %copy-done.8), channel_id=1, source_target_pairs={{0,8},{8,16},{16,24},{24,28},{28,20},{20,12},{12,4},{4,0},{1,9},{9... | collective-permute-start | bytes 614408 | tf_op jit(solution)/shard_map/ppermute | solution.py:485
  98.5 0.2 multiply_reduce_fusion
  98.7 0.2 collective-permute-start.11
  98.8 18.6 %collective-permute-done.10.refs_8_.refs_9_ = bf16[800,128]{1,0:T(8,128)(2,1)S(1)} collective-permute-done((bf16[800,128]{1,0:T(8,128)(2,1)S(1)}, bf16[800,128]{1,0:T(8,128)(2,1)S(1)}, u32[]{:S(2)}, u32[]{:S(2)}) %collective-permute-start.10) | collective-permute-done | bytes 204832 | tf_op jit(solution)/shard_map/ppermute | solution.py:485
  117.4 6.0 %collective-permute-start.12 = (bf16[800,128]{1,0:T(8,128)(2,1)S(1)}, bf16[800,128]{1,0:T(8,128)(2,1)S(1)}, u32[]{:S(2)}, u32[]{:S(2)}) collective-permute-start(bf16[800,128]{1,0:T(8,128)(2,1)S(1)} %collective-permute-done.10.refs_8_.refs_9_), channel_id=1, source_target_pairs={{0,8},{8,16},{16,24},{24,28},{28,20},{20,12},{12,4},{4,0},{1,9},{9... | collective-permute-start | bytes 614408 | tf_op jit(solution)/shard_map/ppermute | solution.py:485
  123.4 0.2 select_reduce_fusion
  123.6 0.7 pad_add_fusion.near_ref
  124.3 7.0 %backward1.1 = (f32[1,128,384]{2,1,0:T(8,128)}, f32[8,384,128]{2,1,0:T(8,128)}, f32[8,384,128]{2,1,0:T(8,128)}) custom-call(s32[8,9]{1,0:T(8,128)} %pad_add_fusion.near_ref, bf16[768,128]{1,0:T(8,128)(2,1)} %get-tuple-element.34.refs_0_, bf16[768,128]{1,0:T(8,128)(2,1)} %copy-done.1, bf16[768,128]{1,0:T(8,128)(2,1)} %copy-done.2, ...), custom_call_target="tpu_custom_call" | custom-call | tf_op jit(solution)/shard_map/backward1/pallas_call | solution.py:490
  131.4 0.1 collective-permute-start.13
  131.5 0.6 copy-done.10
  132.1 9.5 %backward2.1 = (f32[2,128,384]{2,1,0:T(8,128)}, f32[8,384,128]{2,1,0:T(8,128)}, f32[8,384,128]{2,1,0:T(8,128)}) custom-call(s32[8,9]{1,0:T(8,128)} %pad_add_fusion.near_ref, bf16[768,128]{1,0:T(8,128)(2,1)} %get-tuple-element.34.refs_0_, bf16[768,128]{1,0:T(8,128)(2,1)} %copy-done.1, bf16[768,128]{1,0:T(8,128)(2,1)} %copy-done.2, ...), custom_call_target="tpu_custom_call" | custom-call | tf_op jit(solution)/shard_map/backward2/pallas_call | solution.py:490
  141.5 2.5 %collective-permute-start.14 = (bf16[800,128]{1,0:T(8,128)(2,1)S(1)}, bf16[800,128]{1,0:T(8,128)(2,1)S(1)}, u32[]{:S(2)}, u32[]{:S(2)}) collective-permute-start(bf16[800,128]{1,0:T(8,128)(2,1)S(1)} %collective-permute-done.12.refs_8_.refs_11_), channel_id=1, source_target_pairs={{0,8},{8,16},{16,24},{24,28},{28,20},{20,12},{12,4},{4,0},{1,9},{9... | collective-permute-start | bytes 614408 | tf_op jit(solution)/shard_map/ppermute | solution.py:485
  144.0 1.8 fusion.11
  145.9 0.0 collective-permute-start.15
  145.9 0.7 copy-done.12
  146.5 9.3 %backward3.1 = (f32[2,128,384]{2,1,0:T(8,128)}, f32[8,384,128]{2,1,0:T(8,128)}, f32[8,384,128]{2,1,0:T(8,128)}) custom-call(s32[8,9]{1,0:T(8,128)} %pad_add_fusion.near_ref, bf16[768,128]{1,0:T(8,128)(2,1)} %get-tuple-element.34.refs_0_, bf16[768,128]{1,0:T(8,128)(2,1)} %copy-done.1, bf16[768,128]{1,0:T(8,128)(2,1)} %copy-done.2, ...), custom_call_target="tpu_custom_call" | custom-call | tf_op jit(solution)/shard_map/backward3/pallas_call | solution.py:490
  155.8 2.3 %collective-permute-start.16 = (bf16[800,128]{1,0:T(8,128)(2,1)S(1)}, bf16[800,128]{1,0:T(8,128)(2,1)S(1)}, u32[]{:S(2)}, u32[]{:S(2)}) collective-permute-start(bf16[800,128]{1,0:T(8,128)(2,1)S(1)} %collective-permute-done.14.refs_13_), channel_id=1, source_target_pairs={{0,8},{8,16},{16,24},{24,28},{28,20},{20,12},{12,4},{4,0},{1,9},{9... | collective-permute-start | bytes 614408 | tf_op jit(solution)/shard_map/ppermute | solution.py:485
  158.2 1.8 fusion.10
  160.0 0.0 all-gather.6.cloned.1.call-done.refs_24_
  160.0 2.3 %collective-permute-done.16.refs_15_ = bf16[800,128]{1,0:T(8,128)(2,1)S(1)} collective-permute-done((bf16[800,128]{1,0:T(8,128)(2,1)S(1)}, bf16[800,128]{1,0:T(8,128)(2,1)S(1)}, u32[]{:S(2)}, u32[]{:S(2)}) %collective-permute-start.16) | collective-permute-done | bytes 204832 | tf_op jit(solution)/shard_map/ppermute | solution.py:485
  162.4 0.7 copy-done.15
  163.1 17.1 %final.1 = f32[384,384]{1,0:T(8,128)} custom-call(s32[8,9]{1,0:T(8,128)} %pad_add_fusion.near_ref, s32[8]{0:T(128)} %copy-done.21, bf16[768,128]{1,0:T(8,128)(2,1)} %get-tuple-element.34.refs_0_, bf16[768,128]{1,0:T(8,128)(2,1)} %copy-done.1, bf16[768,128]{1,0:T(8,128)(2,1)} %copy-done.2, bf16[768,128]{1,0:T(8,128)(2,1)} %copy-done.3, ...), custom_call_target="tpu_custom_call" | custom-call | tf_op jit(solution)/shard_map/final/pallas_call | solution.py:509
  180.2 0.1 convert_element_type.20
  180.3 0.8 fusion
  (60 shorter events, 0.2 us)
Async XLA Ops:
  7.2 72.6 %all-gather.8.cloned.1.call-start = ((), (), s32[]{:S(2)}) async-start(), calls=%async_computation.3 | async-start | bytes 3932160 | tf_op jit(solution)/shard_map/all_gather | solution.py:379
  7.9 152.1 %all-gather.10.cloned.1.call-start = ((), (), s32[]{:S(2)}) async-start(), calls=%async_computation.4 | async-start | bytes 1843200 | tf_op jit(solution)/shard_map/all_gather | solution.py:422
  7.9 32.5 %copy-start.22 = (s32[8]{0:T(128)S(1)}, s32[8]{0:T(128)}, u32[]{:S(2)}) copy-start(s32[8]{0:T(128)} %param.16) | copy-start | bytes 100
  14.2 8.1 %collective-permute-start = (bf16[768,128]{1,0:T(8,128)(2,1)}, bf16[768,128]{1,0:T(8,128)(2,1)S(1)}, u32[]{:S(2)}, u32[]{:S(2)}) collective-permute-start(bf16[768,128]{1,0:T(8,128)(2,1)} %get-tuple-element.34.refs_0_), channel_id=1, source_target_pairs={{0,8},{8,16},{16,24},{24,28},{28,20},{20,12},{12,4},{4,0},{1,9},{9... | collective-permute-start | bytes 589832 | tf_op jit(solution)/shard_map/ppermute | solution.py:64
  17.2 6.9 %collective-permute-start.1 = (bf16[768,128]{1,0:T(8,128)(2,1)}, bf16[768,128]{1,0:T(8,128)(2,1)S(1)}, u32[]{:S(2)}, u32[]{:S(2)}) collective-permute-start(bf16[768,128]{1,0:T(8,128)(2,1)} %get-tuple-element.34.refs_0_), channel_id=1, source_target_pairs={{0,4},{8,0},{16,8},{24,16},{28,24},{20,28},{12,20},{4,12},{1,5},{9... | collective-permute-start | bytes 589832 | tf_op jit(solution)/shard_map/ppermute | solution.py:66
  22.2 19.1 %copy-start.1 = (bf16[768,128]{1,0:T(8,128)(2,1)}, bf16[768,128]{1,0:T(8,128)(2,1)S(1)}, u32[]{:S(2)}) copy-start(bf16[768,128]{1,0:T(8,128)(2,1)S(1)} %collective-permute-done.refs_1_) | copy-start | bytes 589828
  22.2 6.1 %collective-permute-start.2 = (bf16[768,128]{1,0:T(8,128)(2,1)S(1)}, bf16[768,128]{1,0:T(8,128)(2,1)S(1)}, u32[]{:S(2)}, u32[]{:S(2)}) collective-permute-start(bf16[768,128]{1,0:T(8,128)(2,1)S(1)} %collective-permute-done.refs_1_), channel_id=1, source_target_pairs={{0,8},{8,16},{16,24},{24,28},{28,20},{20,12},{12,4},{4,0},{1,9},{9... | collective-permute-start | bytes 589832 | tf_op jit(solution)/shard_map/ppermute | solution.py:64
  24.0 17.3 %copy-start.2 = (bf16[768,128]{1,0:T(8,128)(2,1)}, bf16[768,128]{1,0:T(8,128)(2,1)S(1)}, u32[]{:S(2)}) copy-start(bf16[768,128]{1,0:T(8,128)(2,1)S(1)} %collective-permute-done.1.refs_2_) | copy-start | bytes 589828
  24.0 5.8 %collective-permute-start.3 = (bf16[768,128]{1,0:T(8,128)(2,1)S(1)}, bf16[768,128]{1,0:T(8,128)(2,1)S(1)}, u32[]{:S(2)}, u32[]{:S(2)}) collective-permute-start(bf16[768,128]{1,0:T(8,128)(2,1)S(1)} %collective-permute-done.1.refs_2_), channel_id=1, source_target_pairs={{0,4},{8,0},{16,8},{24,16},{28,24},{20,28},{12,20},{4,12},{1,5},{9... | collective-permute-start | bytes 589832 | tf_op jit(solution)/shard_map/ppermute | solution.py:66
  28.3 13.0 %copy-start.3 = (bf16[768,128]{1,0:T(8,128)(2,1)}, bf16[768,128]{1,0:T(8,128)(2,1)S(1)}, u32[]{:S(2)}) copy-start(bf16[768,128]{1,0:T(8,128)(2,1)S(1)} %collective-permute-done.2.refs_3_) | copy-start | bytes 589828
  28.3 5.7 %collective-permute-start.4 = (bf16[768,128]{1,0:T(8,128)(2,1)S(1)}, bf16[768,128]{1,0:T(8,128)(2,1)S(1)}, u32[]{:S(2)}, u32[]{:S(2)}) collective-permute-start(bf16[768,128]{1,0:T(8,128)(2,1)S(1)} %collective-permute-done.2.refs_3_), channel_id=1, source_target_pairs={{0,8},{8,16},{16,24},{24,28},{28,20},{20,12},{12,4},{4,0},{1,9},{9... | collective-permute-start | bytes 589832 | tf_op jit(solution)/shard_map/ppermute | solution.py:64
  29.8 11.5 %copy-start.4 = (bf16[768,128]{1,0:T(8,128)(2,1)}, bf16[768,128]{1,0:T(8,128)(2,1)S(1)}, u32[]{:S(2)}) copy-start(bf16[768,128]{1,0:T(8,128)(2,1)S(1)} %collective-permute-done.3.refs_4_) | copy-start | bytes 589828
  29.8 5.7 %collective-permute-start.5 = (bf16[768,128]{1,0:T(8,128)(2,1)S(1)}, bf16[768,128]{1,0:T(8,128)(2,1)S(1)}, u32[]{:S(2)}, u32[]{:S(2)}) collective-permute-start(bf16[768,128]{1,0:T(8,128)(2,1)S(1)} %collective-permute-done.3.refs_4_), channel_id=1, source_target_pairs={{0,4},{8,0},{16,8},{24,16},{28,24},{20,28},{12,20},{4,12},{1,5},{9... | collective-permute-start | bytes 589832 | tf_op jit(solution)/shard_map/ppermute | solution.py:66
  34.0 7.4 %copy-start.5 = (bf16[768,128]{1,0:T(8,128)(2,1)}, bf16[768,128]{1,0:T(8,128)(2,1)S(1)}, u32[]{:S(2)}) copy-start(bf16[768,128]{1,0:T(8,128)(2,1)S(1)} %collective-permute-done.4.refs_5_) | copy-start | bytes 589828
  34.0 5.7 %collective-permute-start.6 = (bf16[768,128]{1,0:T(8,128)(2,1)S(1)}, bf16[768,128]{1,0:T(8,128)(2,1)S(1)}, u32[]{:S(2)}, u32[]{:S(2)}) collective-permute-start(bf16[768,128]{1,0:T(8,128)(2,1)S(1)} %collective-permute-done.4.refs_5_), channel_id=1, source_target_pairs={{0,8},{8,16},{16,24},{24,28},{28,20},{20,12},{12,4},{4,0},{1,9},{9... | collective-permute-start | bytes 589832 | tf_op jit(solution)/shard_map/ppermute | solution.py:64
  35.5 5.9 %copy-start.6 = (bf16[768,128]{1,0:T(8,128)(2,1)}, bf16[768,128]{1,0:T(8,128)(2,1)S(1)}, u32[]{:S(2)}) copy-start(bf16[768,128]{1,0:T(8,128)(2,1)S(1)} %collective-permute-done.5.refs_6_) | copy-start | bytes 589828
  39.7 1.7 copy-start.7
  39.7 120.4 %all-gather.6.cloned.1.call-start = ((), (), s32[]{:S(2)}) async-start(), calls=%async_computation.2 | async-start | bytes 2949120 | tf_op jit(solution)/shard_map/all_gather | solution.py:421
  40.5 7.7 %copy-start.21 = (s32[8]{0:T(128)}, s32[8]{0:T(128)S(1)}, u32[]{:S(2)}) copy-start(s32[8]{0:T(128)S(1)} %dynamic-slice_bitcast_fusion.source_ref) | copy-start | bytes 100
  48.0 24.8 %copy-start.16 = (bf16[384,128]{1,0:T(8,128)(2,1)S(1)}, bf16[384,128]{1,0:T(8,128)(2,1)}, u32[]{:S(2)}) copy-start(bf16[384,128]{1,0:T(8,128)(2,1)} %get-tuple-element.46.refs_0_) | copy-start | bytes 294916
  72.8 1.9 %collective-permute-start.7 = (bf16[384,128]{1,0:T(8,128)(2,1)S(1)}, bf16[384,128]{1,0:T(8,128)(2,1)S(1)}, u32[]{:S(2)}, u32[]{:S(2)}) collective-permute-start(bf16[384,128]{1,0:T(8,128)(2,1)S(1)} %copy-done.16), channel_id=1, source_target_pairs={{0,1},{1,0},{2,3},{3,2},{4,5},{5,4},{6,7},{7,6},{8,9},{9,8},{10,11... | collective-permute-start | bytes 294920 | tf_op jit(solution)/shard_map/ppermute | solution.py:78
  72.9 5.7 %collective-permute-start.8 = (bf16[384,128]{1,0:T(8,128)(2,1)S(1)}, bf16[384,128]{1,0:T(8,128)(2,1)S(1)}, u32[]{:S(2)}, u32[]{:S(2)}) collective-permute-start(bf16[384,128]{1,0:T(8,128)(2,1)S(1)} %copy-done.16), channel_id=1, source_target_pairs={{0,2},{1,3},{2,0},{3,1},{4,6},{5,7},{6,4},{7,5},{8,10},{9,11},{10,... | collective-permute-start | bytes 294920 | tf_op jit(solution)/shard_map/ppermute | solution.py:78
  74.5 5.3 %collective-permute-start.9 = (bf16[384,128]{1,0:T(8,128)(2,1)S(1)}, bf16[384,128]{1,0:T(8,128)(2,1)S(1)}, u32[]{:S(2)}, u32[]{:S(2)}) collective-permute-start(bf16[384,128]{1,0:T(8,128)(2,1)S(1)} %copy-done.16), channel_id=1, source_target_pairs={{0,3},{1,2},{2,1},{3,0},{4,7},{5,6},{6,5},{7,4},{8,11},{9,10},{10,... | collective-permute-start | bytes 294920 | tf_op jit(solution)/shard_map/ppermute | solution.py:78
  74.7 5.0 %copy-start.17 = (bf16[384,128]{1,0:T(8,128)(2,1)}, bf16[384,128]{1,0:T(8,128)(2,1)S(1)}, u32[]{:S(2)}) copy-start(bf16[384,128]{1,0:T(8,128)(2,1)S(1)} %collective-permute-done.7.refs_1_) | copy-start | bytes 294916
  78.5 1.2 copy-start.18
  79.7 0.6 copy-start.19
  89.3 1.9 %copy-start = (f32[128,3072]{1,0:T(8,128)S(1)}, f32[128,3072]{1,0:T(8,128)}, u32[]{:S(2)}) copy-start(f32[128,3072]{1,0:T(8,128)} %get-tuple-element.59) | copy-start | bytes 4718596
  91.5 5.0 %copy-start.8 = (bf16[800,128]{1,0:T(8,128)(2,1)S(1)}, bf16[800,128]{1,0:T(8,128)(2,1)}, u32[]{:S(2)}) copy-start(bf16[800,128]{1,0:T(8,128)(2,1)} %get-tuple-element.47.refs_8_) | copy-start | bytes 614404
  91.5 6.9 %copy-start.20 = (s32[8,8]{1,0:T(8,128)S(1)}, s32[8,8]{1,0:T(8,128)}, u32[]{:S(2)}) copy-start(s32[8,8]{1,0:T(8,128)} %get-tuple-element.67.allowed_ref) | copy-start | bytes 772
  92.7 87.5 %all-to-all-start.1 = ((f16[8,144,384]{2,1,0:T(8,128)(2,1)}), f16[8,144,384]{2,1,0:T(8,128)(2,1)S(1)}, u32[]{:S(2)}, u32[]{:S(2)}) async-start(f16[8,144,384]{2,1,0:T(8,128)(2,1)} %maximum_bitcast_fusion), calls=%async_computation.1 | async-start | bytes 1769472 | tf_op jit(solution)/shard_map/all_to_all | solution.py:472
  96.5 20.8 %collective-permute-start.10 = (bf16[800,128]{1,0:T(8,128)(2,1)S(1)}, bf16[800,128]{1,0:T(8,128)(2,1)S(1)}, u32[]{:S(2)}, u32[]{:S(2)}) collective-permute-start(bf16[800,128]{1,0:T(8,128)(2,1)S(1)} %copy-done.8), channel_id=1, source_target_pairs={{0,8},{8,16},{16,24},{24,28},{28,20},{20,12},{12,4},{4,0},{1,9},{9... | collective-permute-start | bytes 614408 | tf_op jit(solution)/shard_map/ppermute | solution.py:485
  98.7 32.7 %collective-permute-start.11 = (bf16[800,128]{1,0:T(8,128)(2,1)S(1)}, bf16[800,128]{1,0:T(8,128)(2,1)S(1)}, u32[]{:S(2)}, u32[]{:S(2)}) collective-permute-start(bf16[800,128]{1,0:T(8,128)(2,1)S(1)} %copy-done.8), channel_id=1, source_target_pairs={{0,4},{8,0},{16,8},{24,16},{28,24},{20,28},{12,20},{4,12},{1,5},{9... | collective-permute-start | bytes 614408 | tf_op jit(solution)/shard_map/ppermute | solution.py:487
  117.4 14.1 %copy-start.9 = (bf16[800,128]{1,0:T(8,128)(2,1)}, bf16[800,128]{1,0:T(8,128)(2,1)S(1)}, u32[]{:S(2)}) copy-start(bf16[800,128]{1,0:T(8,128)(2,1)S(1)} %collective-permute-done.10.refs_8_.refs_9_) | copy-start | bytes 614404
  117.4 24.1 %collective-permute-start.12 = (bf16[800,128]{1,0:T(8,128)(2,1)S(1)}, bf16[800,128]{1,0:T(8,128)(2,1)S(1)}, u32[]{:S(2)}, u32[]{:S(2)}) collective-permute-start(bf16[800,128]{1,0:T(8,128)(2,1)S(1)} %collective-permute-done.10.refs_8_.refs_9_), channel_id=1, source_target_pairs={{0,8},{8,16},{16,24},{24,28},{28,20},{20,12},{12,4},{4,0},{1,9},{9... | collective-permute-start | bytes 614408 | tf_op jit(solution)/shard_map/ppermute | solution.py:485
  131.4 0.7 copy-start.10
  131.4 14.5 %collective-permute-start.13 = (bf16[800,128]{1,0:T(8,128)(2,1)S(1)}, bf16[800,128]{1,0:T(8,128)(2,1)S(1)}, u32[]{:S(2)}, u32[]{:S(2)}) collective-permute-start(bf16[800,128]{1,0:T(8,128)(2,1)S(1)} %collective-permute-done.11.refs_9_.refs_10_), channel_id=1, source_target_pairs={{0,4},{8,0},{16,8},{24,16},{28,24},{20,28},{12,20},{4,12},{1,5},{9... | collective-permute-start | bytes 614408 | tf_op jit(solution)/shard_map/ppermute | solution.py:487
  141.5 4.3 %copy-start.11 = (bf16[800,128]{1,0:T(8,128)(2,1)}, bf16[800,128]{1,0:T(8,128)(2,1)S(1)}, u32[]{:S(2)}) copy-start(bf16[800,128]{1,0:T(8,128)(2,1)S(1)} %collective-permute-done.12.refs_8_.refs_11_) | copy-start | bytes 614404
  141.5 14.3 %collective-permute-start.14 = (bf16[800,128]{1,0:T(8,128)(2,1)S(1)}, bf16[800,128]{1,0:T(8,128)(2,1)S(1)}, u32[]{:S(2)}, u32[]{:S(2)}) collective-permute-start(bf16[800,128]{1,0:T(8,128)(2,1)S(1)} %collective-permute-done.12.refs_8_.refs_11_), channel_id=1, source_target_pairs={{0,8},{8,16},{16,24},{24,28},{28,20},{20,12},{12,4},{4,0},{1,9},{9... | collective-permute-start | bytes 614408 | tf_op jit(solution)/shard_map/ppermute | solution.py:485
  145.9 0.7 copy-start.12
  145.9 14.1 %collective-permute-start.15 = (bf16[800,128]{1,0:T(8,128)(2,1)S(1)}, bf16[800,128]{1,0:T(8,128)(2,1)S(1)}, u32[]{:S(2)}, u32[]{:S(2)}) collective-permute-start(bf16[800,128]{1,0:T(8,128)(2,1)S(1)} %collective-permute-done.13.refs_9_.refs_12_), channel_id=1, source_target_pairs={{0,4},{8,0},{16,8},{24,16},{28,24},{20,28},{12,20},{4,12},{1,5},{9... | collective-permute-start | bytes 614408 | tf_op jit(solution)/shard_map/ppermute | solution.py:487
  155.8 6.6 %copy-start.13 = (bf16[800,128]{1,0:T(8,128)(2,1)}, bf16[800,128]{1,0:T(8,128)(2,1)S(1)}, u32[]{:S(2)}) copy-start(bf16[800,128]{1,0:T(8,128)(2,1)S(1)} %collective-permute-done.14.refs_13_) | copy-start | bytes 614404
  155.8 6.6 %collective-permute-start.16 = (bf16[800,128]{1,0:T(8,128)(2,1)S(1)}, bf16[800,128]{1,0:T(8,128)(2,1)S(1)}, u32[]{:S(2)}, u32[]{:S(2)}) collective-permute-start(bf16[800,128]{1,0:T(8,128)(2,1)S(1)} %collective-permute-done.14.refs_13_), channel_id=1, source_target_pairs={{0,8},{8,16},{16,24},{24,28},{28,20},{20,12},{12,4},{4,0},{1,9},{9... | collective-permute-start | bytes 614408 | tf_op jit(solution)/shard_map/ppermute | solution.py:485
  160.0 2.4 %copy-start.14 = (bf16[800,128]{1,0:T(8,128)(2,1)}, bf16[800,128]{1,0:T(8,128)(2,1)S(1)}, u32[]{:S(2)}) copy-start(bf16[800,128]{1,0:T(8,128)(2,1)S(1)} %collective-permute-done.15.refs_14_) | copy-start | bytes 614404
  162.4 0.7 copy-start.15
Sparse Core Ops, SparseCore 0:
  9.6 31.2 all-gather.7
  43.0 49.8 all-gather.9
  94.4 22.9 all-gather.5
